TPU v7x, 32 devices: a whole 2x2x4 slice. The times are simulated.
32 devices in a mesh: dom: 16 (over z, y, x), seed: 2 (over core).
Axes of the slice: x: 2, y: 2, z: 4, core: 2. Of those that a mesh axis runs over, the one named last changes fastest.
Arguments:
- rank_in: float32 [128, 262144], P('seed', 'dom'), as said below
- band_tiles: bfloat16 [2048, 3, 128, 128], P('dom'), as said below
- off_tiles: bfloat16 [8192, 128, 128], P('dom'), as said below
- tile_src: int32 [16, 512], P('dom'), may hold values from 0 to 2047, as said below
- tile_row: int32 [16, 512], P('dom'), may hold values from 0 to 127
- tile_count: int32 [16], P('dom'), may hold values from 256 to 512, as said below
- seed_ids: int32 [128], P('seed'), may hold values from 0 to 262143
- dangling: int32 [262144], P('dom'), may hold values 0 or 1
Outputs:
- rank_out: float32 [128, 262144], P('seed', 'dom')
- change: float32 [3, 128], P(None, 'seed')
- total_change: float32 [3], replicated
- seed_score: float32 [128], P('seed')
Inputs may be any that keep to these rules, and one draw needn't show every extreme that they name: `rank_in`: positive. `band_tiles`: nonnegative transition weights. `off_tiles`: nonnegative transition weights. `tile_src`: every source block is held by another index of dom than the tile; the live tiles of one index of dom read at most 2 distinct blocks held by any one other index. The first tile_count[g] slots of index g are live, the rest are padding.
All inputs are finite; a program needn't handle non-finite values. No bound on the sum of `dangling` on one device may be relied on, other than what follows from the above.
Results may differ from a plain program's by a relative error of at most 0.0003.
Values may be sent and summed in bfloat16 or wider, within the bound.
A program may use at most 192 MiB of HBM per device.

v0:
```python
import jax
import jax.numpy as jnp
from jax import lax
from jax.sharding import PartitionSpec as P

CAP = 2
ITERS = 3


DAMP = 0.85


def extended(cells, sides, width):
    for axis, dim in sides:
        count = lax.axis_size(axis)
        ends = count - 1
        head = lax.slice_in_dim(cells, 0, width, axis=dim)
        tail = lax.slice_in_dim(cells, cells.shape[dim] - width, cells.shape[dim], axis=dim)
        cells = jnp.concatenate(
            [
                lax.ppermute(tail, axis, [(i, (i + 1) % count) for i in range(ends)]),
                cells,
                lax.ppermute(head, axis, [((i + 1) % count, i) for i in range(ends)]),
            ],
            axis=dim,
        )
    return cells


def plan_requests(tile_src, tile_count, blocks):
    peer_count = lax.axis_size("dom")
    slot_count = tile_src.shape[1]
    source_ids = tile_src[0]
    live_slots = jnp.arange(slot_count, dtype=jnp.int32) < tile_count[0]
    all_blocks = jnp.arange(blocks * peer_count, dtype=jnp.int32)
    hit_table = jnp.logical_and(source_ids[:, None] == all_blocks[None, :], live_slots[:, None])
    needed = (
        (jnp.sum(hit_table.astype(jnp.int32), axis=0) > 0)
        .astype(jnp.int32)
        .reshape(peer_count, blocks)
    )
    slot_table = jnp.cumsum(needed, axis=1) - 1
    slot_match = needed[:, :, None] * (
        slot_table[:, :, None] == jnp.arange(CAP, dtype=jnp.int32)[None, None, :]
    ).astype(jnp.int32)
    request = jnp.sum(slot_match * jnp.arange(blocks, dtype=jnp.int32)[None, :, None], axis=1)
    wanted = lax.all_to_all(request, "dom", split_axis=0, concat_axis=0, tiled=True)
    holders = source_ids // blocks
    tile_slot = holders * CAP + jnp.take(slot_table.reshape(-1), source_ids)
    tile_slot = jnp.maximum(tile_slot, 0)
    return (wanted, tile_slot, live_slots)


def gather_requested(source, wanted):
    seed_cols, blocks, block_width = source.shape
    peer_count, slots_per = wanted.shape
    outgoing = jnp.take(source, wanted.reshape(-1), axis=1).reshape(
        seed_cols, peer_count, slots_per, block_width
    )
    fetched = lax.all_to_all(outgoing, "dom", split_axis=1, concat_axis=1, tiled=True)
    return fetched.reshape(seed_cols, peer_count * slots_per, block_width)


def on_device(rank_in, band_tiles, off_tiles, tile_src, tile_row, tile_count, seed_ids, dangling):
    blocks = band_tiles.shape[0]
    block_width = band_tiles.shape[2]
    seed_cols = rank_in.shape[0]
    peer_count = lax.axis_size("dom")
    groups = lax.axis_size("seed")
    vertices = blocks * block_width * peer_count
    wanted, tile_slot, live_slots = plan_requests(tile_src, tile_count, blocks)
    tile_rows = jnp.where(live_slots, tile_row[0], blocks)
    first_vertex = lax.axis_index("dom") * (blocks * block_width)
    vertex_ids = first_vertex + jnp.arange(blocks * block_width, dtype=jnp.int32)
    seed_mask = (seed_ids[:, None] == vertex_ids[None, :]).astype(jnp.float32)
    restart = (1.0 - DAMP) * seed_mask
    dead_ends = dangling.astype(jnp.float32)
    keep_share = 1.0 - dead_ends
    rank_now = rank_in
    history = []
    own_total = jnp.zeros((seed_cols,), jnp.float32)
    for iteration in range(ITERS):
        mass_term = jnp.sum(rank_now * dead_ends[None, :], axis=1)
        dead_mass = lax.psum(mass_term, "dom")
        source = (
            (rank_now * keep_share[None, :])
            .astype(jnp.bfloat16)
            .reshape(seed_cols, blocks, block_width)
        )
        padded = extended(source, (("dom", 1),), 1)
        fetched = gather_requested(source, wanted)
        stacked = jnp.stack(
            [padded[:, 0:blocks], padded[:, 1 : blocks + 1], padded[:, 2 : blocks + 2]], axis=2
        )
        banded = jnp.einsum(
            "sbkj,bkij->bsi", stacked, band_tiles, preferred_element_type=jnp.float32
        )
        operands = jnp.take(fetched, tile_slot, axis=1)
        products = jnp.einsum(
            "stj,tij->tsi", operands, off_tiles, preferred_element_type=jnp.float32
        )
        remote = jax.ops.segment_sum(products, tile_rows, num_segments=blocks + 1)[:blocks]
        linked = jnp.transpose(banded + remote, (1, 0, 2)).reshape(seed_cols, blocks * block_width)
        updated = DAMP * (linked + dead_mass[:, None] / vertices) + restart
        gap_here = jnp.sum(jnp.abs(updated - rank_now), axis=1)
        if iteration + 1 < ITERS:
            moved_total = lax.psum(gap_here, "dom")
        else:
            own_here = jnp.sum(updated * seed_mask, axis=1)
            moved_total, own_total = lax.psum((gap_here, own_here), "dom")
        history.append(moved_total / vertices)
        rank_now = updated
    change = jnp.stack(history)
    total_change = lax.psum(jnp.sum(change, axis=1), "seed") / (seed_cols * groups)
    return (rank_now, change, total_change, own_total)


def solution(mesh):
    return jax.shard_map(
        on_device,
        mesh=mesh,
        in_specs=(
            P("seed", "dom"),
            P("dom", None, None, None),
            P("dom", None, None),
            P("dom", None),
            P("dom", None),
            P("dom"),
            P("seed"),
            P("dom"),
        ),
        out_specs=(P("seed", "dom"), P(None, "seed"), P(), P("seed")),
        check_vma=False,
    )
```

profile of v0, /device:TPU:0, one launch (start us, length us, event | category | flops | bytes accessed | tf_op | source)
XLA Modules:
  0.0 638.6 jit_solution(3654220752721472084)
XLA Ops:
  1.3 1.4 convert_reduce_fusion
  2.7 0.3 reduce_window_sum.11
  3.0 0.1 multiply_reduce_fusion.3
  3.1 0.7 copy.53
  3.8 8.3 %all-to-all-start = ((s32[16,1,2]{2,1,0:T(1,128)}), s32[16,1,2]{2,1,0:T(1,128)S(1)}, u32[]{:S(2)}, u32[]{:S(2)}) async-start(s32[16,1,2]{2,1,0:T(1,128)} %copy.53), calls=%async_computation | async-start | bytes 16384 | tf_op jit(solution)/shard_map/all_to_all | solution.py:47
  12.1 0.9 convert_bitcast_fusion.1
  13.0 0.9 broadcast_subtract_fusion
  13.9 4.3 fusion.63
  18.1 0.0 copy-start.1
  18.2 0.0 copy-start.2
  18.2 0.6 copy.79
  18.8 3.8 collective-permute-start
  22.6 1.3 collective-permute-start.1
  24.0 3.1 gather_fusion
  27.1 42.8 %psum.56 = f32[64]{0:T(128)S(1)} all-reduce(f32[64]{0:T(128)S(1)} %get-tuple-element.23), channel_id=1, replica_groups=mesh['dom'=16,'seed'=2] {'dom'}, use_global_device_ids=true, to_apply=%region_5.8 | all-reduce | flops 64 | bytes 512 | tf_op jit(solution)/shard_map/psum | solution.py:84
  69.9 0.5 broadcast.434
  70.5 0.7 reduce.8
  71.1 0.1 reshape.318
  71.3 0.6 gather_fusion.1
  71.9 0.9 broadcast_select_fusion.2
  72.8 3.7 all-to-all-start.1
  76.6 2.2 copy.63
  78.8 2.7 copy.52
  81.5 0.0 collective-permute-done
  81.5 0.0 collective-permute-done.1
  81.5 2.3 fusion.62
  83.8 3.5 all-to-all-done.1
  87.3 13.5 %gather_fusion.2 = bf16[512,64,128]{2,1,0:T(8,128)(2,1)} fusion(bf16[64,32,128]{2,0,1:T(8,128)(2,1)S(1)} %bitcast.126, s32[1024]{0:T(1024)S(1)} %pad_clamp_fusion), kind=kCustom, calls=%fused_computation.1.clone | custom fusion | bytes 16779264 | tf_op jit(solution)/shard_map/jit(_take)/gather | solution.py:98
  100.7 20.4 %fusion.8 = f32[512,64,128]{2,1,0:T(8,128)} fusion(bf16[512,128,128]{2,1,0:T(8,128)(2,1)} %param.14, bf16[512,64,128]{2,1,0:T(8,128)(2,1)} %gather_fusion.2, pred[512]{0:T(512)(128)(4,1)S(1)} %get-tuple-element.15), kind=kOutput, calls=%fused_computation.18 | convolution fusion | flops 1077936128 | bytes 41943552 | tf_op jit(solution)/shard_map/stj,tij->tsi/dot_general | solution.py:99
  121.2 2.5 broadcast.296.clone
  123.7 79.6 %scatter_fusion = f32[129,64,128]{2,1,0:T(8,128)} fusion(f32[129,64,128]{2,1,0:T(8,128)} %broadcast.296.clone, s32[512]{0:T(512)S(1)} %bitcast.134, f32[512,64,128]{2,1,0:T(8,128)} %fusion.8), kind=kCustom, calls=%fused_computation.7 | custom fusion | flops 4194304 | bytes 50333696 | tf_op jit(solution)/shard_map/scatter-add | solution.py:102
  203.3 12.2 %multiply_reduce_fusion.1 = (f32[64]{0:T(128)S(1)}, bf16[64,128,128]{2,0,1:T(8,128)(2,1)S(1)}, f32[128,64,128]{2,1,0:T(8,128)}) fusion(f32[128,128]{1,0:T(8,128)S(1)} %get-tuple-element.38, s32[128,128]{1,0:T(8,128)S(1)} %add_add_fusion, s32[64]{0:T(128)S(1)} %copy-done.3, f32[64]{0:T(128)S(1)} %broadcast_multiply_fusion.3, ...), kind=kOutput, calls=%fused_computation.73 | convolution fusion | flops 822083520 | bytes 29557504 | tf_op jit(solution)/shard_map/sbkj,bkij->bsi/dot_general | solution.py:95
  215.5 0.6 gather_fusion.3
  216.1 0.9 broadcast_select_fusion.1
  217.0 8.5 %all-to-all-start.2 = ((bf16[64,16,2,128]{3,0,2,1:T(8,128)(2,1)}), bf16[64,16,2,128]{3,0,2,1:T(8,128)(2,1)S(1)}, u32[]{:S(2)}, u32[]{:S(2)}) async-start(bf16[64,16,2,128]{3,0,2,1:T(8,128)(2,1)} %bitcast.24), calls=%async_computation.2 | async-start | bytes 1048576 | tf_op jit(solution)/shard_map/all_to_all | solution.py:60
  225.6 3.8 collective-permute-start.2
  229.4 1.3 collective-permute-start.3
  230.7 42.8 %psum.57 = f32[64]{0:T(128)S(1)} all-reduce(f32[64]{0:T(128)S(1)} %get-tuple-element.17), channel_id=1, replica_groups=mesh['dom'=16,'seed'=2] {'dom'}, use_global_device_ids=true, to_apply=%region_8.11 | all-reduce | flops 64 | bytes 512 | tf_op jit(solution)/shard_map/psum | solution.py:84
  273.5 2.2 fusion.60
  275.7 13.5 %gather_fusion.4 = bf16[512,64,128]{2,1,0:T(8,128)(2,1)} fusion(bf16[64,32,128]{2,0,1:T(8,128)(2,1)S(1)} %bitcast.127, s32[1024]{0:T(1024)S(1)} %pad_clamp_fusion), kind=kCustom, calls=%fused_computation.4.clone | custom fusion | bytes 16779264 | tf_op jit(solution)/shard_map/jit(_take)/gather | solution.py:98
  289.2 20.4 %fusion.6 = f32[512,64,128]{2,1,0:T(8,128)} fusion(bf16[512,128,128]{2,1,0:T(8,128)(2,1)} %param.14, bf16[512,64,128]{2,1,0:T(8,128)(2,1)} %gather_fusion.4, pred[512]{0:T(512)(128)(4,1)S(1)} %get-tuple-element.15), kind=kOutput, calls=%fused_computation.16 | convolution fusion | flops 1077936128 | bytes 41943552 | tf_op jit(solution)/shard_map/stj,tij->tsi/dot_general | solution.py:99
  309.6 2.5 broadcast.296.clone.1
  312.1 79.6 %scatter_fusion.1 = f32[129,64,128]{2,1,0:T(8,128)} fusion(f32[129,64,128]{2,1,0:T(8,128)} %broadcast.296.clone.1, s32[512]{0:T(512)S(1)} %bitcast.135, f32[512,64,128]{2,1,0:T(8,128)} %fusion.6), kind=kCustom, calls=%fused_computation.8 | custom fusion | flops 4194304 | bytes 50333696 | tf_op jit(solution)/shard_map/scatter-add | solution.py:102
  391.7 12.0 %multiply_reduce_fusion = (f32[64]{0:T(128)S(1)}, bf16[64,128,128]{2,0,1:T(8,128)(2,1)S(1)}, f32[64,128,128]{2,0,1:T(8,128)}) fusion(f32[128,128]{1,0:T(8,128)S(1)} %get-tuple-element.38, f32[128,128]{1,0:T(8,128)S(1)} %get-tuple-element.41, s32[128,128]{1,0:T(8,128)S(1)} %add_add_fusion, s32[64]{0:T(128)S(1)} %copy-done.3, ...), kind=kOutput, calls=%fused_computation.71 | convolution fusion | flops 822083520 | bytes 29557504 | tf_op jit(solution)/shard_map/sbkj,bkij->bsi/dot_general | solution.py:95
  403.7 0.7 gather_fusion.5
  404.4 0.9 broadcast_select_fusion
  405.3 3.6 all-to-all-start.3
  408.9 3.7 collective-permute-start.4
  412.6 1.3 collective-permute-start.5
  413.9 43.1 %psum.58 = f32[64]{0:T(128)S(1)} all-reduce(f32[64]{0:T(128)S(1)} %get-tuple-element.21), channel_id=1, replica_groups=mesh['dom'=16,'seed'=2] {'dom'}, use_global_device_ids=true, to_apply=%region_11.14 | all-reduce | flops 64 | bytes 512 | tf_op jit(solution)/shard_map/psum | solution.py:84
  457.0 0.0 collective-permute-done.4
  457.0 0.0 collective-permute-done.5
  457.0 2.2 fusion.58
  459.2 0.0 all-to-all-done.3
  459.3 13.5 %gather_fusion.6 = bf16[512,64,128]{2,1,0:T(8,128)(2,1)} fusion(bf16[64,32,128]{2,0,1:T(8,128)(2,1)S(1)} %bitcast.125, s32[1024]{0:T(1024)S(1)} %pad_clamp_fusion), kind=kCustom, calls=%fused_computation.5.clone | custom fusion | bytes 16779264 | tf_op jit(solution)/shard_map/jit(_take)/gather | solution.py:98
  472.7 20.4 %fusion.4 = f32[512,64,128]{2,1,0:T(8,128)} fusion(bf16[512,128,128]{2,1,0:T(8,128)(2,1)} %param.14, bf16[512,64,128]{2,1,0:T(8,128)(2,1)} %gather_fusion.6, pred[512]{0:T(512)(128)(4,1)S(1)} %get-tuple-element.15), kind=kOutput, calls=%fused_computation.14 | convolution fusion | flops 1077936128 | bytes 41943552 | tf_op jit(solution)/shard_map/stj,tij->tsi/dot_general | solution.py:99
  493.2 2.5 broadcast.296
  495.6 79.6 %scatter_fusion.2 = f32[129,64,128]{2,1,0:T(8,128)} fusion(f32[129,64,128]{2,1,0:T(8,128)} %broadcast.296, s32[512]{0:T(512)S(1)} %bitcast.136, f32[512,64,128]{2,1,0:T(8,128)} %fusion.4), kind=kCustom, calls=%fused_computation.9 | custom fusion | flops 4194304 | bytes 50333696 | tf_op jit(solution)/shard_map/scatter-add | solution.py:102
  575.3 14.2 %fusion.35 = (f32[64]{0:T(128)S(1)}, f32[64]{0:T(128)S(1)}, f32[64]{0:T(128)S(1)}, f32[128,64,128]{2,1,0:T(8,128)}) fusion(f32[64]{0:T(128)S(1)} %broadcast_multiply_fusion.1, s32[128,128]{1,0:T(8,128)S(1)} %add_add_fusion, s32[64]{0:T(128)S(1)} %copy-done.3, f32[64,128,128]{2,0,1:T(8,128)} %get-tuple-element.45, f32[64]{0:T(128)S(1)} %broadcast_multiply_fusion.3, ...), kind=kOutput, calls=%fused_computation.51 | convolution fusion | flops 829423424 | bytes 35718656 | tf_op jit(solution)/shard_map/sbkj,bkij->bsi/dot_general | solution.py:95
  589.5 7.0 %fusion.34 = (f32[64]{0:T(128)S(1)}, f32[64,16384]{1,0:T(8,128)}) fusion(f32[64,16384]{1,0:T(8,128)} %param.12, f32[64]{0:T(128)S(1)} %broadcast_multiply_fusion.3, s32[16384]{0:T(1024)S(1)} %iota_add_fusion, s32[64]{0:T(128)S(1)} %copy-done.3, f32[64]{0:T(128)S(1)} %broadcast_multiply_fusion.1, f32[128,64,128]{2,1,0:T(8,128)} %get-tuple-element.46, ...), kind=kLoop, calls=%fused_computation.50 | loop fusion | flops 11534272 | bytes 16843776 | tf_op jit(solution)/shard_map/reduce_sum | solution.py:105
  596.4 38.1 %all-reduce = (f32[64]{0:T(128)S(1)}, f32[64]{0:T(128)S(1)}, f32[64]{0:T(128)S(1)}, f32[64]{0:T(128)}) all-reduce(f32[64]{0:T(128)S(1)} %get-tuple-element.7, f32[64]{0:T(128)S(1)} %get-tuple-element.8, f32[64]{0:T(128)S(1)} %get-tuple-element.36, f32[64]{0:T(128)S(1)} %get-tuple-element.6), channel_id=1, replica_groups=mesh['dom'=16,'seed'=2] {'dom'}, use_global_device_ids=true, to_apply=%region_17.20 | all-reduce | flops 256 | bytes 2048 | tf_op jit(solution)/shard_map/psum | solution.py:110
  634.5 0.7 fusion.78
  635.2 2.5 psum.62
  637.6 0.5 broadcast_multiply_fusion
  (31 shorter events, 0.2 us)
Async XLA Ops:
  3.8 66.1 %all-to-all-start = ((s32[16,1,2]{2,1,0:T(1,128)}), s32[16,1,2]{2,1,0:T(1,128)S(1)}, u32[]{:S(2)}, u32[]{:S(2)}) async-start(s32[16,1,2]{2,1,0:T(1,128)} %copy.53), calls=%async_computation | async-start | bytes 16384 | tf_op jit(solution)/shard_map/all_to_all | solution.py:47
  18.1 5.8 copy-start.1
  18.2 58.4 %copy-start.2 = (s32[1,512]{1,0:T(1,128)S(1)}, s32[1,512]{1,0:T(1,128)}, u32[]{:S(2)}) copy-start(s32[1,512]{1,0:T(1,128)} %param.16) | copy-start | bytes 6148
  18.8 62.7 %collective-permute-start = (bf16[64,1,128]{2,0,1:T(8,128)(2,1)S(1)}, bf16[64,1,128]{2,0,1:T(8,128)(2,1)S(1)}, u32[]{:S(2)}, u32[]{:S(2)}) collective-permute-start(bf16[64,1,128]{2,0,1:T(8,128)(2,1)S(1)} %get-tuple-element.34), channel_id=1, source_target_pairs={{0,2},{2,4},{4,6},{6,8},{8,10},{10,12},{12,14},{14,16},{16,18},{18... | collective-permute-start | bytes 49160 | tf_op jit(solution)/shard_map/ppermute | solution.py:21
  22.6 58.9 %collective-permute-start.1 = (bf16[64,1,128]{2,0,1:T(8,128)(2,1)S(1)}, bf16[64,1,128]{2,0,1:T(8,128)(2,1)S(1)}, u32[]{:S(2)}, u32[]{:S(2)}) collective-permute-start(bf16[64,1,128]{2,0,1:T(8,128)(2,1)S(1)} %get-tuple-element.35), channel_id=1, source_target_pairs={{2,0},{4,2},{6,4},{8,6},{10,8},{12,10},{14,12},{16,14},{18,16},{20... | collective-permute-start | bytes 49160 | tf_op jit(solution)/shard_map/ppermute | solution.py:23
  72.8 14.5 %all-to-all-start.1 = ((bf16[64,16,2,128]{3,0,2,1:T(8,128)(2,1)}), bf16[64,16,2,128]{3,0,2,1:T(8,128)(2,1)S(1)}, u32[]{:S(2)}, u32[]{:S(2)}) async-start(bf16[64,16,2,128]{3,0,2,1:T(8,128)(2,1)} %bitcast.14), calls=%async_computation.1 | async-start | bytes 1048576 | tf_op jit(solution)/shard_map/all_to_all | solution.py:60
  123.7 79.6 %copy-start.3 = (s32[64]{0:T(128)S(1)}, s32[64]{0:T(128)}, u32[]{:S(2)}) copy-start(s32[64]{0:T(128)} %param.18) | copy-start | bytes 772
  215.5 60.3 %copy-start = (bf16[64,128,128]{2,0,1:T(8,128)(2,1)}, bf16[64,128,128]{2,0,1:T(8,128)(2,1)S(1)}, u32[]{:S(2)}) copy-start(bf16[64,128,128]{2,0,1:T(8,128)(2,1)S(1)} %get-tuple-element.18) | copy-start | bytes 6291460
  217.0 58.7 %all-to-all-start.2 = ((bf16[64,16,2,128]{3,0,2,1:T(8,128)(2,1)}), bf16[64,16,2,128]{3,0,2,1:T(8,128)(2,1)S(1)}, u32[]{:S(2)}, u32[]{:S(2)}) async-start(bf16[64,16,2,128]{3,0,2,1:T(8,128)(2,1)} %bitcast.24), calls=%async_computation.2 | async-start | bytes 1048576 | tf_op jit(solution)/shard_map/all_to_all | solution.py:60
  225.6 47.9 %collective-permute-start.2 = (bf16[64,1,128]{2,0,1:T(8,128)(2,1)S(1)}, bf16[64,1,128]{2,0,1:T(8,128)(2,1)S(1)}, u32[]{:S(2)}, u32[]{:S(2)}) collective-permute-start(bf16[64,1,128]{2,0,1:T(8,128)(2,1)S(1)} %get-tuple-element.30), channel_id=1, source_target_pairs={{0,2},{2,4},{4,6},{6,8},{8,10},{10,12},{12,14},{14,16},{16,18},{18... | collective-permute-start | bytes 49160 | tf_op jit(solution)/shard_map/ppermute | solution.py:21
  229.4 44.1 %collective-permute-start.3 = (bf16[64,1,128]{2,0,1:T(8,128)(2,1)S(1)}, bf16[64,1,128]{2,0,1:T(8,128)(2,1)S(1)}, u32[]{:S(2)}, u32[]{:S(2)}) collective-permute-start(bf16[64,1,128]{2,0,1:T(8,128)(2,1)S(1)} %get-tuple-element.31), channel_id=1, source_target_pairs={{2,0},{4,2},{6,4},{8,6},{10,8},{12,10},{14,12},{16,14},{18,16},{20... | collective-permute-start | bytes 49160 | tf_op jit(solution)/shard_map/ppermute | solution.py:23
  405.3 54.0 %all-to-all-start.3 = ((bf16[64,16,2,128]{3,0,2,1:T(8,128)(2,1)}), bf16[64,16,2,128]{3,0,2,1:T(8,128)(2,1)S(1)}, u32[]{:S(2)}, u32[]{:S(2)}) async-start(bf16[64,16,2,128]{3,0,2,1:T(8,128)(2,1)} %bitcast.34), calls=%async_computation.3 | async-start | bytes 1048576 | tf_op jit(solution)/shard_map/all_to_all | solution.py:60
  408.9 48.1 %collective-permute-start.4 = (bf16[64,1,128]{2,0,1:T(8,128)(2,1)S(1)}, bf16[64,1,128]{2,0,1:T(8,128)(2,1)S(1)}, u32[]{:S(2)}, u32[]{:S(2)}) collective-permute-start(bf16[64,1,128]{2,0,1:T(8,128)(2,1)S(1)} %get-tuple-element.26), channel_id=1, source_target_pairs={{0,2},{2,4},{4,6},{6,8},{8,10},{10,12},{12,14},{14,16},{16,18},{18... | collective-permute-start | bytes 49160 | tf_op jit(solution)/shard_map/ppermute | solution.py:21
  412.6 44.4 %collective-permute-start.5 = (bf16[64,1,128]{2,0,1:T(8,128)(2,1)S(1)}, bf16[64,1,128]{2,0,1:T(8,128)(2,1)S(1)}, u32[]{:S(2)}, u32[]{:S(2)}) collective-permute-start(bf16[64,1,128]{2,0,1:T(8,128)(2,1)S(1)} %get-tuple-element.27), channel_id=1, source_target_pairs={{2,0},{4,2},{6,4},{8,6},{10,8},{12,10},{14,12},{16,14},{18,16},{20... | collective-permute-start | bytes 49160 | tf_op jit(solution)/shard_map/ppermute | solution.py:23
where the time goes:
time: 648 us; the launch traced here: 639 us
  other arithmetic  265 us (41%)
  blocking collectives  169 us (26%)
  matrix products  99.6 us (15%)
  local copies, waits for them, and re-layouts  59.6 us (9%)
  starting transfers between devices  39.4 us (6%)
    scatter-add x3, other arithmetic, on_device(): jax.ops.segment_sum(products, tile_rows, num_segments=blocks + 1)[:blocks]  239 us
    psum x3, blocking collectives, on_device(): dead_mass = lax.psum(mass_term, 'dom')  129 us
    dot_general x3, matrix products, on_device(): jnp.einsum('stj,tij->tsi', operands, off_tiles, preferred_element_type=jn...  61.3 us
    gather x3, local copies, waits for them, and re-layouts, on_device(): operands = jnp.take(fetched, tile_slot, axis=1)  40.4 us
    dot_general x3, matrix products, on_device(): jnp.einsum('sbkj,bkij->bsi', stacked, band_tiles, preferred_element_type=...  38.3 us
    psum x1, blocking collectives, on_device(): moved_total, own_total = lax.psum((gap_here, own_here), 'dom')  38.1 us
    all_to_all x3, starting transfers between devices, gather_requested(): lax.all_to_all(outgoing, 'dom', split_axis=1, concat_axis=1, tiled=True)  15.8 us
  transfers between devices with their start and end apart: 10, of which 1 were waited for; matrix products, arithmetic and copies ran while one was open for 4% of the time, Pallas kernels for 0%

commit v1 on v0

v1 whole, which is shorter than its diff:
```python
import functools

import jax
import jax.numpy as jnp
from jax import lax
from jax.experimental import pallas as pl
from jax.experimental.pallas import tpu as pltpu
from jax.sharding import PartitionSpec as P

CAP = 2
ITERS = 3
DAMP = 0.85
LANES = 128
STAT_ROWS = 8
GROUP = 16
CHUNKS = 8
VMEM_BYTES = 60 * 1024 * 1024
MESH = pl.DeviceIdType.MESH
WHOLE = pl.BlockSpec(memory_space=pltpu.VMEM)
SCALARS = pl.BlockSpec(memory_space=pltpu.SMEM)
FAR = pl.BlockSpec(memory_space=pl.ANY)


def dot_nt(a, b):
    return lax.dot_general(a, b, (((1,), (1,)), ((), ())), preferred_element_type=jnp.float32)


def greet_all(count, me):
    barrier = pltpu.get_barrier_semaphore()

    @pl.loop(1, count)
    def _(d):
        pl.semaphore_signal(
            barrier, inc=1, device_id={"dom": lax.rem(me + d, count)}, device_id_type=MESH
        )

    pl.semaphore_wait(barrier, count - 1)


def columns_to_rows(columns, seed_cols):
    lane = lax.broadcasted_iota(jnp.int32, (seed_cols, LANES), 1)
    tile = jnp.zeros((seed_cols, LANES), jnp.float32)
    for k, column in enumerate(columns):
        tile = jnp.where(lane == k, column, tile)
    square = jnp.concatenate([tile, jnp.zeros((LANES - seed_cols, LANES), jnp.float32)], axis=0)
    return square.T[:STAT_ROWS]


def row_to_column(rows, seed_cols):
    square = jnp.concatenate(
        [rows, jnp.zeros((LANES - rows.shape[0], LANES), jnp.float32)], axis=0
    )
    return square.T[:seed_cols, 0:1]


def bcast_kernel(count, stat_ref, all_ref, send_sem, recv_sem):
    me = lax.axis_index("dom")
    greet_all(count, me)

    def copy(d):
        return pltpu.make_async_remote_copy(
            src_ref=stat_ref,
            dst_ref=all_ref.at[me],
            send_sem=send_sem.at[d],
            recv_sem=recv_sem.at[d],
            device_id={"dom": lax.rem(me + d, count)},
            device_id_type=MESH,
        )

    @pl.loop(1, count)
    def _(d):
        copy(d).start()

    all_ref[me] = stat_ref[...]

    @pl.loop(1, count)
    def _(d):
        copy(d).wait()


def bcast(stat, count):
    return pl.pallas_call(
        functools.partial(bcast_kernel, count),
        out_shape=jax.ShapeDtypeStruct((count,) + stat.shape, stat.dtype),
        in_specs=[WHOLE],
        out_specs=WHOLE,
        scratch_shapes=[pltpu.SemaphoreType.DMA((count,)), pltpu.SemaphoreType.DMA((count,))],
        compiler_params=pltpu.CompilerParams(collective_id=1, has_side_effects=True),
        name="bcast_stats",
    )(stat)


def exchange_kernel(
    count, wanted_ref, src_ref, stat_ref, fetched_ref, halo_ref, all_ref,
    staging, block_send, block_recv, stat_send, stat_recv, halo_send, halo_recv,
):
    me = lax.axis_index("dom")
    blocks = src_ref.shape[0]
    greet_all(count, me)

    def block_copy(d):
        peer = lax.rem(me + d, count)
        return pltpu.make_async_remote_copy(
            src_ref=staging.at[peer],
            dst_ref=fetched_ref.at[me],
            send_sem=block_send.at[d],
            recv_sem=block_recv.at[d],
            device_id={"dom": peer},
            device_id_type=MESH,
        )

    def stat_copy(d):
        return pltpu.make_async_remote_copy(
            src_ref=stat_ref,
            dst_ref=all_ref.at[me],
            send_sem=stat_send.at[d],
            recv_sem=stat_recv.at[d],
            device_id={"dom": lax.rem(me + d, count)},
            device_id_type=MESH,
        )

    def halo_copy(side):
        step = 1 if side == 0 else count - 1
        return pltpu.make_async_remote_copy(
            src_ref=src_ref.at[blocks - 1 if side == 0 else 0],
            dst_ref=halo_ref.at[side],
            send_sem=halo_send.at[side],
            recv_sem=halo_recv.at[side],
            device_id={"dom": lax.rem(me + step, count)},
            device_id_type=MESH,
        )

    @pl.loop(1, count)
    def _(d):
        peer = lax.rem(me + d, count)
        for c in range(CAP):
            staging[peer, c] = src_ref[wanted_ref[peer * CAP + c]]
        block_copy(d).start()

    halo_copy(0).start()
    halo_copy(1).start()

    @pl.loop(1, count)
    def _(d):
        stat_copy(d).start()

    fetched_ref[me] = jnp.zeros(fetched_ref.shape[1:], fetched_ref.dtype)
    all_ref[me] = stat_ref[...]
    halo_copy(0).wait()
    halo_copy(1).wait()

    @pl.loop(1, count)
    def _(d):
        block_copy(d).wait()
        stat_copy(d).wait()


def exchange(wanted, src, stat, count):
    block = src.shape[1:]
    sems = lambda k: [pltpu.SemaphoreType.DMA((k,)), pltpu.SemaphoreType.DMA((k,))]
    return pl.pallas_call(
        functools.partial(exchange_kernel, count),
        out_shape=(
            jax.ShapeDtypeStruct((count, CAP) + block, src.dtype),
            jax.ShapeDtypeStruct((2,) + block, src.dtype),
            jax.ShapeDtypeStruct((count,) + stat.shape, stat.dtype),
        ),
        in_specs=[SCALARS, WHOLE, WHOLE],
        out_specs=(WHOLE, WHOLE, WHOLE),
        scratch_shapes=[pltpu.VMEM((count, CAP) + block, src.dtype)]
        + sems(count) + sems(count) + sems(2),
        compiler_params=pltpu.CompilerParams(
            collective_id=0, has_side_effects=True, vmem_limit_bytes=VMEM_BYTES // 2
        ),
        name="exchange_blocks",
    )(wanted, src, stat)


def init_kernel(rank_ref, dang_ref, src_ref, stat_ref):
    blocks, seed_cols, width = src_ref.shape

    def step(b, mass):
        dead = dang_ref[pl.ds(b, 1), :].astype(jnp.float32)
        rank = rank_ref[:, pl.ds(pl.multiple_of(b * width, width), width)]
        src_ref[b] = (rank * (1.0 - dead)).astype(src_ref.dtype)
        return mass + rank * dead

    mass = lax.fori_loop(0, blocks, step, jnp.zeros((seed_cols, width), jnp.float32), unroll=4)
    stat_ref[...] = columns_to_rows([jnp.sum(mass, axis=1, keepdims=True)], seed_cols)


def init(rank, dang, blocks, width):
    return pl.pallas_call(
        init_kernel,
        out_shape=(
            jax.ShapeDtypeStruct((blocks, rank.shape[0], width), jnp.bfloat16),
            jax.ShapeDtypeStruct((STAT_ROWS, LANES), jnp.float32),
        ),
        in_specs=[WHOLE, WHOLE],
        out_specs=(WHOLE, WHOLE),
        compiler_params=pltpu.CompilerParams(vmem_limit_bytes=VMEM_BYTES // 2),
        name="first_source",
    )(rank, dang)


def step_kernel(
    vertices, slot_ref, row_ref, place_ref, band_hbm, off_hbm, rank_ref, src_ref, fetched_ref,
    halo_ref, all_ref, dang_ref, seed_ref, rank_out, src_out, stat_out,
    band, off, ext, acc, band_sem, off_sem,
):
    blocks, seed_cols, width = src_ref.shape
    slots = off.shape[0]
    band_part = blocks // CHUNKS
    off_part = slots // CHUNKS
    live = place_ref[0]
    me = place_ref[1]
    last = place_ref[2]

    def band_copy(c):
        part = pl.ds(c * band_part, band_part)
        return pltpu.make_async_copy(band_hbm.at[part], band.at[part], band_sem.at[c])

    def off_copy(c):
        part = pl.ds(c * off_part, off_part)
        return pltpu.make_async_copy(off_hbm.at[part], off.at[part], off_sem.at[c])

    for c in range(CHUNKS):
        band_copy(c).start()
    for c in range(CHUNKS):
        off_copy(c).start()

    zero = jnp.zeros((seed_cols, width), ext.dtype)
    ext[0] = jnp.where(me > 0, halo_ref[0], zero)
    ext[blocks + 1] = jnp.where(me < last, halo_ref[1], zero)

    def fill(b, carry):
        ext[b + 1] = src_ref[b]
        return carry

    lax.fori_loop(0, blocks, fill, 0, unroll=8)

    @pl.loop(0, CHUNKS)
    def _(c):
        band_copy(c).wait()

        def one(i, carry):
            b = c * band_part + i
            pair = jnp.concatenate([ext[b], ext[b + 1]], axis=1)
            tiles = jnp.concatenate([band[b, 0], band[b, 1]], axis=1)
            acc[b] = dot_nt(pair, tiles) + dot_nt(ext[b + 2], band[b, 2])
            return carry

        lax.fori_loop(0, band_part, one, 0, unroll=4)

    @pl.loop(0, CHUNKS)
    def _(c):
        off_copy(c).wait()

        @pl.loop(0, off_part // GROUP)
        def _(g):
            base = c * off_part + g * GROUP

            @pl.when(base < live)
            def _():
                products = [
                    dot_nt(fetched_ref[slot_ref[base + u]], off[base + u]) for u in range(GROUP)
                ]
                for u in range(GROUP):
                    row = row_ref[base + u]
                    acc[row] = acc[row] + products[u]

    mass = row_to_column(jnp.sum(all_ref[...], axis=0), seed_cols) / vertices
    mass = jnp.broadcast_to(mass, (seed_cols, width))
    seeds = jnp.broadcast_to(seed_ref[...], (seed_cols, width)) - me * (blocks * width)
    lane = lax.broadcasted_iota(jnp.int32, (seed_cols, width), 1)
    seeds = seeds - lane

    def finish(b, carry):
        dead_mass, moved, own = carry
        here = pl.ds(pl.multiple_of(b * width, width), width)
        dead = dang_ref[pl.ds(b, 1), :].astype(jnp.float32)
        is_seed = seeds == b * width
        rank = rank_ref[:, here]
        updated = DAMP * (acc[b] + mass) + jnp.where(is_seed, 1.0 - DAMP, 0.0)
        rank_out[:, here] = updated
        src_out[b] = (updated * (1.0 - dead)).astype(src_out.dtype)
        return (
            dead_mass + updated * dead,
            moved + jnp.abs(updated - rank),
            own + jnp.where(is_seed, updated, 0.0),
        )

    nothing = jnp.zeros((seed_cols, width), jnp.float32)
    sums = lax.fori_loop(0, blocks, finish, (nothing, nothing, nothing), unroll=2)
    stat_out[...] = columns_to_rows([jnp.sum(s, axis=1, keepdims=True) for s in sums], seed_cols)


def step(vertices, slot, row, place, band, off, rank, src, fetched, halo, stats, dang, seeds):
    blocks, seed_cols, width = src.shape
    flops = 2 * seed_cols * width * width * (3 * blocks + off.shape[0])
    return pl.pallas_call(
        functools.partial(step_kernel, vertices),
        out_shape=(
            jax.ShapeDtypeStruct(rank.shape, rank.dtype),
            jax.ShapeDtypeStruct(src.shape, src.dtype),
            jax.ShapeDtypeStruct((STAT_ROWS, LANES), jnp.float32),
        ),
        in_specs=[SCALARS, SCALARS, SCALARS, FAR, FAR] + [WHOLE] * 7,
        out_specs=(WHOLE, WHOLE, WHOLE),
        scratch_shapes=[
            pltpu.VMEM(band.shape, band.dtype),
            pltpu.VMEM(off.shape, off.dtype),
            pltpu.VMEM((blocks + 2, seed_cols, width), src.dtype),
            pltpu.VMEM((blocks + 1, seed_cols, width), jnp.float32),
            pltpu.SemaphoreType.DMA((CHUNKS,)),
            pltpu.SemaphoreType.DMA((CHUNKS,)),
        ],
        compiler_params=pltpu.CompilerParams(vmem_limit_bytes=VMEM_BYTES),
        cost_estimate=pl.CostEstimate(
            flops=flops, bytes_accessed=2 * (band.size + off.size), transcendentals=0
        ),
        name="power_step",
    )(slot, row, place, band, off, rank, src, fetched, halo, stats, dang, seeds)


def plan_requests(tile_src, tile_count, blocks, count):
    source = tile_src[0]
    live = jnp.arange(source.shape[0], dtype=jnp.int32) < tile_count[0]
    holder = source // blocks
    inside = source - holder * blocks
    held = holder[None, :] == jnp.arange(count, dtype=jnp.int32)[:, None]
    read = jnp.logical_and(held, live[None, :])
    low = jnp.min(jnp.where(read, inside[None, :], blocks - 1), axis=1)
    high = jnp.max(jnp.where(read, inside[None, :], 0), axis=1)
    tile_low = jnp.sum(jnp.where(held, low[:, None], 0), axis=0)
    slot = holder * CAP + (inside != tile_low).astype(jnp.int32)
    return jnp.stack([low, high], axis=1).reshape(-1), slot, live


def on_device(rank_in, band_tiles, off_tiles, tile_src, tile_row, tile_count, seed_ids, dangling):
    blocks = band_tiles.shape[0]
    width = band_tiles.shape[2]
    seed_cols = rank_in.shape[0]
    count = lax.axis_size("dom")
    groups = lax.axis_size("seed")
    vertices = blocks * width * count
    me = lax.axis_index("dom")

    requests, slot, live = plan_requests(tile_src, tile_count, blocks, count)
    rows = jnp.where(live, tile_row[0], blocks)
    padded = jnp.pad(requests, (0, STAT_ROWS * LANES - count * CAP)).reshape(STAT_ROWS, LANES)
    asked = bcast(padded.astype(jnp.float32), count)
    asked = asked.reshape(count, STAT_ROWS * LANES)
    wanted = lax.dynamic_slice_in_dim(asked, me * CAP, CAP, axis=1)
    wanted = wanted.astype(jnp.int32).reshape(-1)

    dang = dangling.reshape(blocks, width)
    seeds = seed_ids[:, None]
    place = jnp.stack([tile_count[0], me.astype(jnp.int32), jnp.int32(count - 1)])
    rank = rank_in
    src, stat = init(rank, dang, blocks, width)
    gathered = []
    for _ in range(ITERS):
        fetched, halo, stats = exchange(wanted, src, stat, count)
        gathered.append(stats)
        fetched = fetched.reshape((count * CAP,) + src.shape[1:])
        rank, src, stat = step(
            vertices, slot, rows, place, band_tiles, off_tiles, rank, src, fetched, halo, stats,
            dang, seeds,
        )
    gathered.append(bcast(stat, count))
    moved = jnp.stack([jnp.sum(g[:, 1, :seed_cols], axis=0) for g in gathered[1:]])
    own = jnp.sum(gathered[-1][:, 2, :seed_cols], axis=0)
    change = moved / vertices
    total_change = lax.psum(jnp.sum(change, axis=1), "seed") / (seed_cols * groups)
    return (rank, change, total_change, own)


def solution(mesh):
    return jax.shard_map(
        on_device,
        mesh=mesh,
        in_specs=(
            P("seed", "dom"),
            P("dom", None, None, None),
            P("dom", None, None),
            P("dom", None),
            P("dom", None),
            P("dom"),
            P("seed"),
            P("dom"),
        ),
        out_specs=(P("seed", "dom"), P(None, "seed"), P(), P("seed")),
        check_vma=False,
    )
```

time: 648 us -> 206 us (0.32); the launches traced: 639 us -> 207 us
  other arithmetic: 265 us -> 7.98 us
  Pallas kernels: 0 us -> 179 us
  blocking collectives: 169 us -> 2.46 us
  matrix products: 99.6 us -> 0 us
  local copies, waits for them, and re-layouts: 59.6 us -> 16.1 us
  starting transfers between devices: 39.4 us -> 0 us
    scatter-add x3 -> x0, other arithmetic: 239 us -> none  [on_device(): jax.ops.segment_sum(products, tile_rows, num_segments=blocks + 1)[:blocks]]
    pallas_call x0 -> x9, Pallas kernels: none -> 179 us  [the longest x3 84.7 us: step(): pl.pallas_call(functools.partial(step_kernel, vertices), out_shape=(jax.S...]
    psum x4 -> x0, blocking collectives: 167 us -> none  [the longest x3 129 us: on_device(): dead_mass = lax.psum(mass_term, 'dom')]
    dot_general x6 -> x0, matrix products: 99.6 us -> none  [the longest x3 61.3 us: on_device(): jnp.einsum('stj,tij->tsi', operands, off_tiles, preferred_element_type=jn...]
    gather x7 -> x0, local copies, waits for them, and re-layouts: 45.5 us -> none  [the longest x3 40.4 us: on_device(): operands = jnp.take(fetched, tile_slot, axis=1)]
    all_to_all x4 -> x0, starting transfers between devices: 24.1 us -> none  [the longest x3 15.8 us: gather_requested(): lax.all_to_all(outgoing, 'dom', split_axis=1, concat_axis=1, tiled=True)]
    ppermute x6 -> x0, starting transfers between devices: 15.2 us -> none  [the longest x3 11.4 us: extended(): lax.ppermute(tail, axis, [(i, (i + 1) % count) for i in range(ends)])]
    unnamed x9 -> x33, local copies, waits for them, and re-layouts: 2.18 us -> 14.5 us
  transfers between devices with their start and end apart: 10 -> 0, of which waited for: 1 -> 0; matrix products, arithmetic and copies ran while one was open for 4% -> 0% of each run, Pallas kernels for 0% -> 0%
where the time goes in v1:
time: 206 us; the launch traced here: 207 us
  Pallas kernels  179 us (87%)
  local copies, waits for them, and re-layouts  16.1 us (8%)
  other arithmetic  7.98 us (4%)
  blocking collectives  2.46 us (1%)
    pallas_call x3, Pallas kernels, step(): pl.pallas_call(functools.partial(step_kernel, vertices), out_shape=(jax.S...  84.7 us
    pallas_call x3, Pallas kernels, exchange(): pl.pallas_call(functools.partial(exchange_kernel, count), out_shape=(jax....  67.8 us
    pallas_call x2, Pallas kernels, bcast(): pl.pallas_call(functools.partial(bcast_kernel, count), out_shape=jax.Shap...  25.5 us
    unnamed x33, local copies, waits for them, and re-layouts  14.5 us

profile of v1, /device:TPU:0, one launch (start us, length us, event | category | flops | bytes accessed | tf_op | source)
XLA Modules:
  0.0 206.9 jit_solution(1947623778541606666)
XLA Ops:
  1.3 0.7 pad_add_fusion.1.place_ref
  1.9 0.7 multiply_subtract_fusion
  2.6 0.1 select_reduce_fusion
  2.8 0.1 select_reduce_fusion.1
  2.9 1.3 convert_add_fusion
  4.2 0.1 copy.20
  4.2 0.1 reshape.37
  4.3 0.6 convert_bitcast_fusion.stat_ref
  4.9 1.3 copy.21.seed_ref
  6.3 11.1 %bcast_stats.2 = f32[16,8,128]{2,1,0:T(8,128)} custom-call(f32[8,128]{1,0:T(8,128)} %convert_bitcast_fusion.stat_ref), custom_call_target="tpu_custom_call" | custom-call | tf_op jit(solution)/shard_map/bcast_stats/pallas_call | solution.py:82
  17.4 0.9 copy.26
  18.2 0.1 dynamic-slice_convert_fusion
  18.3 0.1 reshape.39.wanted_ref
  18.4 0.0 copy-start
  18.4 2.2 %copy-done = f32[64,16384]{1,0:T(8,128)S(1)} copy-done((f32[64,16384]{1,0:T(8,128)S(1)}, f32[64,16384]{1,0:T(8,128)}, u32[]{:S(2)}) %copy-start) | copy-done | bytes 4194328
  20.6 0.0 copy-start.4
  20.6 0.8 copy-done.4
  21.4 0.8 first_source.1
  22.2 0.0 copy-start.3
  22.2 19.2 %exchange_blocks.3 = (bf16[16,2,64,128]{3,2,1,0:T(8,128)(2,1)S(1)}, bf16[2,64,128]{2,1,0:T(8,128)(2,1)S(1)}, f32[16,8,128]{2,1,0:T(8,128)S(1)}) custom-call(s32[32]{0:T(128)S(1)} %reshape.39.wanted_ref, bf16[128,64,128]{2,1,0:T(8,128)(2,1)S(1)} %get-tuple-element.23.src_ref, f32[8,128]{1,0:T(8,128)S(1)} %get-tuple-element.24.stat_ref), custom_call_target="tpu_custom_call" | custom-call | tf_op jit(solution)/shard_map/exchange_blocks/pallas_call | solution.py:161
  41.4 0.0 copy-start.7
  41.4 0.8 copy-done.7
  42.2 0.0 copy-start.10
  42.2 0.6 copy-done.10
  42.8 0.0 copy-start.13
  42.8 0.6 copy-done.13
  43.4 0.0 copy-done.3
  43.4 28.3 %power_step.3 = (f32[64,16384]{1,0:T(8,128)}, bf16[128,64,128]{2,1,0:T(8,128)(2,1)}, f32[8,128]{1,0:T(8,128)}) custom-call(s32[512]{0:T(512)} %get-tuple-element.50.slot_ref, s32[512]{0:T(512)} %get-tuple-element.51.row_ref, s32[3]{0:T(128)} %pad_add_fusion.1.place_ref, bf16[128,3,128,128]{3,2,1,0:T(8,128)(2,1)} %band_hbm.5, bf16[512,128,128]{2,1,0:T(8,128)(2,1)} %off_hbm.5, ...), custom_call_target="tpu_custom_call" | custom-call | flops 1879048192 | bytes 29360128 | tf_op jit(solution)/shard_map/power_step/pallas_call | solution.py:301
  71.7 0.0 copy-start.2
  71.7 1.6 copy-done.2
  73.3 0.0 copy-start.15
  73.3 0.7 copy-done.15
  74.0 25.0 %exchange_blocks.4 = (bf16[16,2,64,128]{3,2,1,0:T(8,128)(2,1)S(1)}, bf16[2,64,128]{2,1,0:T(8,128)(2,1)S(1)}, f32[16,8,128]{2,1,0:T(8,128)S(1)}) custom-call(s32[32]{0:T(128)S(1)} %reshape.39.wanted_ref, bf16[128,64,128]{2,1,0:T(8,128)(2,1)S(1)} %copy-done.2, f32[8,128]{1,0:T(8,128)S(1)} %copy-done.15), custom_call_target="tpu_custom_call" | custom-call | tf_op jit(solution)/shard_map/exchange_blocks/pallas_call | solution.py:161
  99.0 0.0 copy-start.6
  99.0 0.8 copy-done.6
  99.9 0.0 copy-start.9
  99.9 0.6 copy-done.9
  100.5 0.0 copy-start.12
  100.5 0.6 copy-done.12
  101.1 28.2 %power_step.4 = (f32[64,16384]{1,0:T(8,128)}, bf16[128,64,128]{2,1,0:T(8,128)(2,1)}, f32[8,128]{1,0:T(8,128)}) custom-call(s32[512]{0:T(512)} %get-tuple-element.50.slot_ref, s32[512]{0:T(512)} %get-tuple-element.51.row_ref, s32[3]{0:T(128)} %pad_add_fusion.1.place_ref, bf16[128,3,128,128]{3,2,1,0:T(8,128)(2,1)} %band_hbm.5, bf16[512,128,128]{2,1,0:T(8,128)(2,1)} %off_hbm.5, ...), custom_call_target="tpu_custom_call" | custom-call | flops 1879048192 | bytes 29360128 | tf_op jit(solution)/shard_map/power_step/pallas_call | solution.py:301
  129.3 0.9 slice_reduce_fusion.3
  130.2 0.0 copy-start.1
  130.2 1.6 copy-done.1
  131.8 0.0 copy-start.14
  131.8 0.7 copy-done.14
  132.4 23.6 %exchange_blocks.5 = (bf16[16,2,64,128]{3,2,1,0:T(8,128)(2,1)S(1)}, bf16[2,64,128]{2,1,0:T(8,128)(2,1)S(1)}, f32[16,8,128]{2,1,0:T(8,128)S(1)}) custom-call(s32[32]{0:T(128)S(1)} %reshape.39.wanted_ref, bf16[128,64,128]{2,1,0:T(8,128)(2,1)S(1)} %copy-done.1, f32[8,128]{1,0:T(8,128)S(1)} %copy-done.14), custom_call_target="tpu_custom_call" | custom-call | tf_op jit(solution)/shard_map/exchange_blocks/pallas_call | solution.py:161
  156.0 0.0 copy-start.5
  156.1 0.8 copy-done.5
  156.9 0.0 copy-start.8
  156.9 0.6 copy-done.8
  157.5 0.0 copy-start.11
  157.5 0.6 copy-done.11
  158.1 28.3 %power_step.5 = (f32[64,16384]{1,0:T(8,128)}, bf16[128,64,128]{2,1,0:T(8,128)(2,1)}, f32[8,128]{1,0:T(8,128)}) custom-call(s32[512]{0:T(512)} %get-tuple-element.50.slot_ref, s32[512]{0:T(512)} %get-tuple-element.51.row_ref, s32[3]{0:T(128)} %pad_add_fusion.1.place_ref, bf16[128,3,128,128]{3,2,1,0:T(8,128)(2,1)} %band_hbm.5, bf16[512,128,128]{2,1,0:T(8,128)(2,1)} %off_hbm.5, ...), custom_call_target="tpu_custom_call" | custom-call | flops 1879048192 | bytes 29360128 | tf_op jit(solution)/shard_map/power_step/pallas_call | solution.py:301
  186.4 0.9 slice_reduce_fusion.2
  187.3 14.5 %bcast_stats.3 = f32[16,8,128]{2,1,0:T(8,128)} custom-call(f32[8,128]{1,0:T(8,128)} %get-tuple-element.41.stat_ref), custom_call_target="tpu_custom_call" | custom-call | tf_op jit(solution)/shard_map/bcast_stats/pallas_call | solution.py:82
  201.7 1.5 slice_reduce_fusion
  203.2 0.7 fusion.3
  203.9 2.5 %psum.7 = f32[3]{0:T(128)S(1)} all-reduce(f32[3]{0:T(128)S(1)} %get-tuple-element.46), channel_id=1, replica_groups=mesh['dom'=16,'seed'=2] {'seed'}, use_global_device_ids=true, to_apply=%region_7.8 | all-reduce | flops 3 | bytes 24 | tf_op jit(solution)/shard_map/psum | solution.py:375
  206.4 0.5 broadcast_multiply_fusion
  (2 shorter events, 0.0 us)
Async XLA Ops:
  18.4 2.2 %copy-start = (f32[64,16384]{1,0:T(8,128)S(1)}, f32[64,16384]{1,0:T(8,128)}, u32[]{:S(2)}) copy-start(f32[64,16384]{1,0:T(8,128)} %rank_ref.3) | copy-start | bytes 12582916
  20.6 0.8 copy-start.4
  22.2 21.2 %copy-start.3 = (bf16[128,64,128]{2,1,0:T(8,128)(2,1)}, bf16[128,64,128]{2,1,0:T(8,128)(2,1)S(1)}, u32[]{:S(2)}) copy-start(bf16[128,64,128]{2,1,0:T(8,128)(2,1)S(1)} %get-tuple-element.23.src_ref) | copy-start | bytes 6291460
  41.4 0.8 copy-start.7
  42.2 0.6 copy-start.10
  42.8 0.6 copy-start.13
  71.7 1.6 copy-start.2
  73.3 0.7 copy-start.15
  99.0 0.9 copy-start.6
  99.9 0.6 copy-start.9
  100.5 0.6 copy-start.12
  130.2 1.6 copy-start.1
  131.8 0.7 copy-start.14
  156.0 0.9 copy-start.5
  156.9 0.6 copy-start.8
  157.5 0.6 copy-start.11

commit v2 on v1

--- a/solution.py
+++ b/solution.py
@@ -14,11 +14,13 @@
 STAT_ROWS = 8
 GROUP = 16
 CHUNKS = 8
-VMEM_BYTES = 60 * 1024 * 1024
+EARLY = 1
+STEP_BYTES = 36 * 1024 * 1024
+EXCHANGE_BYTES = 36 * 1024 * 1024
 MESH = pl.DeviceIdType.MESH
 WHOLE = pl.BlockSpec(memory_space=pltpu.VMEM)
 SCALARS = pl.BlockSpec(memory_space=pltpu.SMEM)
-FAR = pl.BlockSpec(memory_space=pl.ANY)
+FAR = pl.BlockSpec(memory_space=pltpu.HBM)
 
 
 def dot_nt(a, b):
@@ -26,6 +28,11 @@
 
 
 def greet_all(count, me):
+    signal_all(count, me)
+    pl.semaphore_wait(pltpu.get_barrier_semaphore(), count - 1)
+
+
+def signal_all(count, me):
     barrier = pltpu.get_barrier_semaphore()
 
     @pl.loop(1, count)
@@ -33,8 +40,6 @@
         pl.semaphore_signal(
             barrier, inc=1, device_id={"dom": lax.rem(me + d, count)}, device_id_type=MESH
         )
-
-    pl.semaphore_wait(barrier, count - 1)
 
 
 def columns_to_rows(columns, seed_cols):
@@ -91,12 +96,37 @@
 
 
 def exchange_kernel(
-    count, wanted_ref, src_ref, stat_ref, fetched_ref, halo_ref, all_ref,
-    staging, block_send, block_recv, stat_send, stat_recv, halo_send, halo_recv,
+    count, wanted_ref, src_ref, stat_ref, band_hbm, fetched_ref, all_ref, part_ref,
+    band, halo, band_sem, staging, block_send, block_recv, stat_send, stat_recv, halo_send, halo_recv,
 ):
     me = lax.axis_index("dom")
     blocks = src_ref.shape[0]
-    greet_all(count, me)
+    band_part = blocks // CHUNKS
+    signal_all(count, me)
+
+    def band_copy(c):
+        part = pl.ds(c * band_part, band_part)
+        return pltpu.make_async_copy(band_hbm.at[part], band.at[part], band_sem.at[c])
+
+    for c in range(CHUNKS):
+        band_copy(c).start()
+
+    def banded(b, left, middle, right):
+        pair = jnp.concatenate([left, middle], axis=1)
+        tiles = jnp.concatenate([band[b, 0], band[b, 1]], axis=1)
+        part_ref[b] = dot_nt(pair, tiles) + dot_nt(right, band[b, 2])
+
+    def band_chunk(c):
+        band_copy(c).wait()
+
+        def one(i, carry):
+            b = c * band_part + i
+            left = jnp.maximum(b - 1, 0)
+            right = jnp.minimum(b + 1, blocks - 1)
+            banded(b, src_ref[left], src_ref[b], src_ref[right])
+            return carry
+
+        lax.fori_loop(0, band_part, one, 0, unroll=4)
 
     def block_copy(d):
         peer = lax.rem(me + d, count)
@@ -123,7 +153,7 @@
         step = 1 if side == 0 else count - 1
         return pltpu.make_async_remote_copy(
             src_ref=src_ref.at[blocks - 1 if side == 0 else 0],
-            dst_ref=halo_ref.at[side],
+            dst_ref=halo.at[side],
             send_sem=halo_send.at[side],
             recv_sem=halo_recv.at[side],
             device_id={"dom": lax.rem(me + step, count)},
@@ -135,6 +165,15 @@
         peer = lax.rem(me + d, count)
         for c in range(CAP):
             staging[peer, c] = src_ref[wanted_ref[peer * CAP + c]]
+
+    fetched_ref[me] = jnp.zeros(fetched_ref.shape[1:], fetched_ref.dtype)
+    all_ref[me] = stat_ref[...]
+    for c in range(EARLY):
+        band_chunk(c)
+    pl.semaphore_wait(pltpu.get_barrier_semaphore(), count - 1)
+
+    @pl.loop(1, count)
+    def _(d):
         block_copy(d).start()
 
     halo_copy(0).start()
@@ -144,10 +183,16 @@
     def _(d):
         stat_copy(d).start()
 
-    fetched_ref[me] = jnp.zeros(fetched_ref.shape[1:], fetched_ref.dtype)
-    all_ref[me] = stat_ref[...]
+    @pl.loop(EARLY, CHUNKS)
+    def _(c):
+        band_chunk(c)
+
     halo_copy(0).wait()
     halo_copy(1).wait()
+    zero = jnp.zeros(halo.shape[1:], halo.dtype)
+    banded(0, jnp.where(me > 0, halo[0], zero), src_ref[0], src_ref[1])
+    end = blocks - 1
+    banded(end, src_ref[end - 1], src_ref[end], jnp.where(me < count - 1, halo[1], zero))
 
     @pl.loop(1, count)
     def _(d):
@@ -155,25 +200,34 @@
         stat_copy(d).wait()
 
 
-def exchange(wanted, src, stat, count):
+def exchange(wanted, src, stat, band, count):
     block = src.shape[1:]
+    flops = 2 * block[0] * block[1] * block[1] * 3 * src.shape[0]
     sems = lambda k: [pltpu.SemaphoreType.DMA((k,)), pltpu.SemaphoreType.DMA((k,))]
     return pl.pallas_call(
         functools.partial(exchange_kernel, count),
         out_shape=(
             jax.ShapeDtypeStruct((count, CAP) + block, src.dtype),
-            jax.ShapeDtypeStruct((2,) + block, src.dtype),
             jax.ShapeDtypeStruct((count,) + stat.shape, stat.dtype),
-        ),
-        in_specs=[SCALARS, WHOLE, WHOLE],
+            jax.ShapeDtypeStruct(src.shape, jnp.float32),
+        ),
+        in_specs=[SCALARS, WHOLE, WHOLE, FAR],
         out_specs=(WHOLE, WHOLE, WHOLE),
-        scratch_shapes=[pltpu.VMEM((count, CAP) + block, src.dtype)]
+        scratch_shapes=[
+            pltpu.VMEM(band.shape, band.dtype),
+            pltpu.VMEM((2,) + block, src.dtype),
+            pltpu.SemaphoreType.DMA((CHUNKS,)),
+            pltpu.VMEM((count, CAP) + block, src.dtype),
+        ]
         + sems(count) + sems(count) + sems(2),
         compiler_params=pltpu.CompilerParams(
-            collective_id=0, has_side_effects=True, vmem_limit_bytes=VMEM_BYTES // 2
+            collective_id=0, has_side_effects=True, vmem_limit_bytes=EXCHANGE_BYTES
+        ),
+        cost_estimate=pl.CostEstimate(
+            flops=flops, bytes_accessed=2 * band.size, transcendentals=0
         ),
         name="exchange_blocks",
-    )(wanted, src, stat)
+    )(wanted, src, stat, band)
 
 
 def init_kernel(rank_ref, dang_ref, src_ref, stat_ref):
@@ -198,59 +252,33 @@
         ),
         in_specs=[WHOLE, WHOLE],
         out_specs=(WHOLE, WHOLE),
-        compiler_params=pltpu.CompilerParams(vmem_limit_bytes=VMEM_BYTES // 2),
+        compiler_params=pltpu.CompilerParams(vmem_limit_bytes=EXCHANGE_BYTES),
         name="first_source",
     )(rank, dang)
 
 
 def step_kernel(
-    vertices, slot_ref, row_ref, place_ref, band_hbm, off_hbm, rank_ref, src_ref, fetched_ref,
-    halo_ref, all_ref, dang_ref, seed_ref, rank_out, src_out, stat_out,
-    band, off, ext, acc, band_sem, off_sem,
+    vertices, slot_ref, row_ref, place_ref, off_hbm, rank_ref, part_ref, fetched_ref,
+    all_ref, dang_ref, seed_ref, rank_out, src_out, stat_out, off, acc, off_sem,
 ):
-    blocks, seed_cols, width = src_ref.shape
+    blocks, seed_cols, width = part_ref.shape
     slots = off.shape[0]
-    band_part = blocks // CHUNKS
     off_part = slots // CHUNKS
     live = place_ref[0]
     me = place_ref[1]
-    last = place_ref[2]
-
-    def band_copy(c):
-        part = pl.ds(c * band_part, band_part)
-        return pltpu.make_async_copy(band_hbm.at[part], band.at[part], band_sem.at[c])
 
     def off_copy(c):
         part = pl.ds(c * off_part, off_part)
         return pltpu.make_async_copy(off_hbm.at[part], off.at[part], off_sem.at[c])
 
     for c in range(CHUNKS):
-        band_copy(c).start()
-    for c in range(CHUNKS):
         off_copy(c).start()
 
-    zero = jnp.zeros((seed_cols, width), ext.dtype)
-    ext[0] = jnp.where(me > 0, halo_ref[0], zero)
-    ext[blocks + 1] = jnp.where(me < last, halo_ref[1], zero)
-
     def fill(b, carry):
-        ext[b + 1] = src_ref[b]
+        acc[b] = part_ref[b]
         return carry
 
-    lax.fori_loop(0, blocks, fill, 0, unroll=8)
-
-    @pl.loop(0, CHUNKS)
-    def _(c):
-        band_copy(c).wait()
-
-        def one(i, carry):
-            b = c * band_part + i
-            pair = jnp.concatenate([ext[b], ext[b + 1]], axis=1)
-            tiles = jnp.concatenate([band[b, 0], band[b, 1]], axis=1)
-            acc[b] = dot_nt(pair, tiles) + dot_nt(ext[b + 2], band[b, 2])
-            return carry
-
-        lax.fori_loop(0, band_part, one, 0, unroll=4)
+    lax.fori_loop(0, blocks, fill, 0, unroll=4)
 
     @pl.loop(0, CHUNKS)
     def _(c):
@@ -295,32 +323,29 @@
     stat_out[...] = columns_to_rows([jnp.sum(s, axis=1, keepdims=True) for s in sums], seed_cols)
 
 
-def step(vertices, slot, row, place, band, off, rank, src, fetched, halo, stats, dang, seeds):
-    blocks, seed_cols, width = src.shape
-    flops = 2 * seed_cols * width * width * (3 * blocks + off.shape[0])
+def step(vertices, slot, row, place, off, rank, part, fetched, stats, dang, seeds):
+    blocks, seed_cols, width = part.shape
+    flops = 2 * seed_cols * width * width * off.shape[0]
     return pl.pallas_call(
         functools.partial(step_kernel, vertices),
         out_shape=(
             jax.ShapeDtypeStruct(rank.shape, rank.dtype),
-            jax.ShapeDtypeStruct(src.shape, src.dtype),
+            jax.ShapeDtypeStruct(part.shape, fetched.dtype),
             jax.ShapeDtypeStruct((STAT_ROWS, LANES), jnp.float32),
         ),
-        in_specs=[SCALARS, SCALARS, SCALARS, FAR, FAR] + [WHOLE] * 7,
+        in_specs=[SCALARS, SCALARS, SCALARS, FAR] + [WHOLE] * 6,
         out_specs=(WHOLE, WHOLE, WHOLE),
         scratch_shapes=[
-            pltpu.VMEM(band.shape, band.dtype),
             pltpu.VMEM(off.shape, off.dtype),
-            pltpu.VMEM((blocks + 2, seed_cols, width), src.dtype),
             pltpu.VMEM((blocks + 1, seed_cols, width), jnp.float32),
             pltpu.SemaphoreType.DMA((CHUNKS,)),
-            pltpu.SemaphoreType.DMA((CHUNKS,)),
         ],
-        compiler_params=pltpu.CompilerParams(vmem_limit_bytes=VMEM_BYTES),
+        compiler_params=pltpu.CompilerParams(vmem_limit_bytes=STEP_BYTES),
         cost_estimate=pl.CostEstimate(
-            flops=flops, bytes_accessed=2 * (band.size + off.size), transcendentals=0
+            flops=flops, bytes_accessed=2 * off.size, transcendentals=0
         ),
         name="power_step",
-    )(slot, row, place, band, off, rank, src, fetched, halo, stats, dang, seeds)
+    )(slot, row, place, off, rank, part, fetched, stats, dang, seeds)
 
 
 def plan_requests(tile_src, tile_count, blocks, count):
@@ -356,17 +381,16 @@
 
     dang = dangling.reshape(blocks, width)
     seeds = seed_ids[:, None]
-    place = jnp.stack([tile_count[0], me.astype(jnp.int32), jnp.int32(count - 1)])
+    place = jnp.stack([tile_count[0], me.astype(jnp.int32)])
     rank = rank_in
     src, stat = init(rank, dang, blocks, width)
     gathered = []
     for _ in range(ITERS):
-        fetched, halo, stats = exchange(wanted, src, stat, count)
+        fetched, stats, part = exchange(wanted, src, stat, band_tiles, count)
         gathered.append(stats)
         fetched = fetched.reshape((count * CAP,) + src.shape[1:])
         rank, src, stat = step(
-            vertices, slot, rows, place, band_tiles, off_tiles, rank, src, fetched, halo, stats,
-            dang, seeds,
+            vertices, slot, rows, place, off_tiles, rank, part, fetched, stats, dang, seeds
         )
     gathered.append(bcast(stat, count))
     moved = jnp.stack([jnp.sum(g[:, 1, :seed_cols], axis=0) for g in gathered[1:]])

time: 206 us -> 152 us (0.74)
  Pallas kernels: 179 us -> 139 us
  local copies, waits for them, and re-layouts: 16.1 us -> 5.43 us
  other arithmetic: 7.98 us -> 5.14 us
    pallas_call x3, Pallas kernels: 84.7 us -> 44.8 us  [step(): pl.pallas_call(functools.partial(step_kernel, vertices), out_shape=(jax.S...]
    unnamed x33 -> x9, local copies, waits for them, and re-layouts: 14.5 us -> 4.43 us
where the time goes in v2:
time: 152 us; the launch traced here: 153 us
  Pallas kernels  139 us (91%)
  local copies, waits for them, and re-layouts  5.43 us (4%)
  other arithmetic  5.14 us (3%)
  blocking collectives  2.46 us (2%)
    pallas_call x3, Pallas kernels, exchange(): pl.pallas_call(functools.partial(exchange_kernel, count), out_shape=(jax....  67.2 us
    pallas_call x3, Pallas kernels, step(): pl.pallas_call(functools.partial(step_kernel, vertices), out_shape=(jax.S...  44.8 us
    pallas_call x2, Pallas kernels, bcast(): pl.pallas_call(functools.partial(bcast_kernel, count), out_shape=jax.Shap...  26 us
    unnamed x9, local copies, waits for them, and re-layouts  4.43 us

profile of v2, /device:TPU:0, one launch (start us, length us, event | category | flops | bytes accessed | tf_op | source)
XLA Modules:
  0.0 153.2 jit_solution(13763963756531157490)
XLA Ops:
  1.3 0.1 pad_add_fusion.1.place_ref
  1.4 0.7 multiply_subtract_fusion
  2.1 0.1 select_reduce_fusion
  2.2 0.1 select_reduce_fusion.1
  2.3 0.7 convert_add_fusion
  3.0 0.1 copy.20
  3.1 0.1 reshape.36
  3.2 0.6 convert_bitcast_fusion.stat_ref
  3.8 0.7 copy.21.seed_ref
  4.5 11.1 %bcast_stats.2 = f32[16,8,128]{2,1,0:T(8,128)} custom-call(f32[8,128]{1,0:T(8,128)} %convert_bitcast_fusion.stat_ref), custom_call_target="tpu_custom_call" | custom-call | tf_op jit(solution)/shard_map/bcast_stats/pallas_call | solution.py:87
  15.6 0.9 copy.26
  16.5 0.1 dynamic-slice_convert_fusion
  16.5 0.1 reshape.38.wanted_ref
  16.6 0.0 copy-start
  16.6 2.2 %copy-done = f32[64,16384]{1,0:T(8,128)S(1)} copy-done((f32[64,16384]{1,0:T(8,128)S(1)}, f32[64,16384]{1,0:T(8,128)}, u32[]{:S(2)}) %copy-start) | copy-done | bytes 4194328
  18.8 0.0 copy-start.2
  18.8 0.8 copy-done.2
  19.7 0.8 first_source.1
  20.5 0.0 copy-start.1
  20.5 20.9 %exchange_blocks.3 = (bf16[16,2,64,128]{3,2,1,0:T(8,128)(2,1)S(1)}, f32[16,8,128]{2,1,0:T(8,128)S(1)}, f32[128,64,128]{2,1,0:T(8,128)S(1)}) custom-call(s32[32]{0:T(128)S(1)} %reshape.38.wanted_ref, bf16[128,64,128]{2,1,0:T(8,128)(2,1)S(1)} %get-tuple-element.23.src_ref, f32[8,128]{1,0:T(8,128)S(1)} %get-tuple-element.24.stat_ref, ...), custom_call_target="tpu_custom_call" | custom-call | flops 805306368 | bytes 12582912 | tf_op jit(solution)/shard_map/exchange_blocks/pallas_call | solution.py:207
  41.4 0.0 copy-done.1
  41.4 14.1 %power_step.3 = (f32[64,16384]{1,0:T(8,128)S(1)}, bf16[128,64,128]{2,1,0:T(8,128)(2,1)S(1)}, f32[8,128]{1,0:T(8,128)S(1)}) custom-call(s32[512]{0:T(512)S(1)} %get-tuple-element.50.slot_ref, s32[512]{0:T(512)S(1)} %get-tuple-element.51.row_ref, s32[2]{0:T(128)S(1)} %pad_add_fusion.1.place_ref, bf16[512,128,128]{2,1,0:T(8,128)(2,1)} %off_hbm.5, ...), custom_call_target="tpu_custom_call" | custom-call | flops 1073741824 | bytes 16777216 | tf_op jit(solution)/shard_map/power_step/pallas_call | solution.py:329
  55.5 22.3 %exchange_blocks.4 = (bf16[16,2,64,128]{3,2,1,0:T(8,128)(2,1)S(1)}, f32[16,8,128]{2,1,0:T(8,128)S(1)}, f32[128,64,128]{2,1,0:T(8,128)S(1)}) custom-call(s32[32]{0:T(128)S(1)} %reshape.38.wanted_ref, bf16[128,64,128]{2,1,0:T(8,128)(2,1)S(1)} %get-tuple-element.29.src_ref, f32[8,128]{1,0:T(8,128)S(1)} %get-tuple-element.30.stat_ref, ...), custom_call_target="tpu_custom_call" | custom-call | flops 805306368 | bytes 12582912 | tf_op jit(solution)/shard_map/exchange_blocks/pallas_call | solution.py:207
  77.8 14.1 %power_step.4 = (f32[64,16384]{1,0:T(8,128)S(1)}, bf16[128,64,128]{2,1,0:T(8,128)(2,1)S(1)}, f32[8,128]{1,0:T(8,128)S(1)}) custom-call(s32[512]{0:T(512)S(1)} %get-tuple-element.50.slot_ref, s32[512]{0:T(512)S(1)} %get-tuple-element.51.row_ref, s32[2]{0:T(128)S(1)} %pad_add_fusion.1.place_ref, bf16[512,128,128]{2,1,0:T(8,128)(2,1)} %off_hbm.5, ...), custom_call_target="tpu_custom_call" | custom-call | flops 1073741824 | bytes 16777216 | tf_op jit(solution)/shard_map/power_step/pallas_call | solution.py:329
  92.0 23.9 %exchange_blocks.5 = (bf16[16,2,64,128]{3,2,1,0:T(8,128)(2,1)S(1)}, f32[16,8,128]{2,1,0:T(8,128)S(1)}, f32[128,64,128]{2,1,0:T(8,128)S(1)}) custom-call(s32[32]{0:T(128)S(1)} %reshape.38.wanted_ref, bf16[128,64,128]{2,1,0:T(8,128)(2,1)S(1)} %get-tuple-element.35.src_ref, f32[8,128]{1,0:T(8,128)S(1)} %get-tuple-element.36.stat_ref, ...), custom_call_target="tpu_custom_call" | custom-call | flops 805306368 | bytes 12582912 | tf_op jit(solution)/shard_map/exchange_blocks/pallas_call | solution.py:207
  115.9 16.6 %power_step.5 = (f32[64,16384]{1,0:T(8,128)}, bf16[128,64,128]{2,1,0:T(8,128)(2,1)}, f32[8,128]{1,0:T(8,128)S(1)}) custom-call(s32[512]{0:T(512)S(1)} %get-tuple-element.50.slot_ref, s32[512]{0:T(512)S(1)} %get-tuple-element.51.row_ref, s32[2]{0:T(128)S(1)} %pad_add_fusion.1.place_ref, bf16[512,128,128]{2,1,0:T(8,128)(2,1)} %off_hbm.5, ...), custom_call_target="tpu_custom_call" | custom-call | flops 1073741824 | bytes 16777216 | tf_op jit(solution)/shard_map/power_step/pallas_call | solution.py:329
  132.6 0.0 copy-start.3
  132.6 0.5 copy-done.3
  133.2 14.9 %bcast_stats.3 = f32[16,8,128]{2,1,0:T(8,128)} custom-call(f32[8,128]{1,0:T(8,128)} %copy-done.3), custom_call_target="tpu_custom_call" | custom-call | tf_op jit(solution)/shard_map/bcast_stats/pallas_call | solution.py:87
  148.1 1.5 slice_reduce_fusion
  149.5 0.7 fusion.3
  150.2 2.5 %psum.7 = f32[3]{0:T(128)S(1)} all-reduce(f32[3]{0:T(128)S(1)} %get-tuple-element.46), channel_id=1, replica_groups=mesh['dom'=16,'seed'=2] {'seed'}, use_global_device_ids=true, to_apply=%region_7.8 | all-reduce | flops 3 | bytes 24 | tf_op jit(solution)/shard_map/psum | solution.py:399
  152.7 0.5 broadcast_multiply_fusion
  (4 shorter events, 0.1 us)
Async XLA Ops:
  16.6 2.2 %copy-start = (f32[64,16384]{1,0:T(8,128)S(1)}, f32[64,16384]{1,0:T(8,128)}, u32[]{:S(2)}) copy-start(f32[64,16384]{1,0:T(8,128)} %rank_ref.3) | copy-start | bytes 12582916
  18.8 0.8 copy-start.2
  20.5 20.9 %copy-start.1 = (f32[64,16384]{1,0:T(8,128)S(1)}, f32[64,16384]{1,0:T(8,128)}, u32[]{:S(2)}) copy-start(f32[64,16384]{1,0:T(8,128)} %rank_ref.3) | copy-start | bytes 12582916
  132.6 0.6 copy-start.3

commit v3 on v2

--- a/solution.py
+++ b/solution.py
@@ -12,10 +12,11 @@
 DAMP = 0.85
 LANES = 128
 STAT_ROWS = 8
-GROUP = 16
+GROUP = 32
 CHUNKS = 8
 EARLY = 1
 STEP_BYTES = 36 * 1024 * 1024
+FIRST_BYTES = 48 * 1024 * 1024
 EXCHANGE_BYTES = 36 * 1024 * 1024
 MESH = pl.DeviceIdType.MESH
 WHOLE = pl.BlockSpec(memory_space=pltpu.VMEM)
@@ -27,11 +28,6 @@
     return lax.dot_general(a, b, (((1,), (1,)), ((), ())), preferred_element_type=jnp.float32)
 
 
-def greet_all(count, me):
-    signal_all(count, me)
-    pl.semaphore_wait(pltpu.get_barrier_semaphore(), count - 1)
-
-
 def signal_all(count, me):
     barrier = pltpu.get_barrier_semaphore()
 
@@ -45,7 +41,7 @@
 def columns_to_rows(columns, seed_cols):
     lane = lax.broadcasted_iota(jnp.int32, (seed_cols, LANES), 1)
     tile = jnp.zeros((seed_cols, LANES), jnp.float32)
-    for k, column in enumerate(columns):
+    for k, column in columns.items():
         tile = jnp.where(lane == k, column, tile)
     square = jnp.concatenate([tile, jnp.zeros((LANES - seed_cols, LANES), jnp.float32)], axis=0)
     return square.T[:STAT_ROWS]
@@ -58,14 +54,27 @@
     return square.T[:seed_cols, 0:1]
 
 
-def bcast_kernel(count, stat_ref, all_ref, send_sem, recv_sem):
+def first_kernel(
+    count, request_ref, dang_ref, rank_hbm, asked_ref, src_ref, mass_ref,
+    rank, rank_sem, send_sem, recv_sem,
+):
     me = lax.axis_index("dom")
-    greet_all(count, me)
+    blocks, seed_cols, width = src_ref.shape
+    part = blocks // CHUNKS
+    signal_all(count, me)
+
+    def rank_copy(c):
+        here = pl.ds(c * part * width, part * width)
+        return pltpu.make_async_copy(rank_hbm.at[:, here], rank.at[:, here], rank_sem.at[c])
+
+    for c in range(CHUNKS):
+        rank_copy(c).start()
+    pl.semaphore_wait(pltpu.get_barrier_semaphore(), count - 1)
 
     def copy(d):
         return pltpu.make_async_remote_copy(
-            src_ref=stat_ref,
-            dst_ref=all_ref.at[me],
+            src_ref=request_ref,
+            dst_ref=asked_ref.at[me],
             send_sem=send_sem.at[d],
             recv_sem=recv_sem.at[d],
             device_id={"dom": lax.rem(me + d, count)},
@@ -76,22 +85,110 @@
     def _(d):
         copy(d).start()
 
-    all_ref[me] = stat_ref[...]
+    asked_ref[me] = request_ref[...]
+    mass_ref[...] = jnp.zeros(mass_ref.shape, mass_ref.dtype)
+
+    @pl.loop(0, CHUNKS)
+    def _(c):
+        rank_copy(c).wait()
+
+        def one(i, mass):
+            b = c * part + i
+            dead = dang_ref[pl.ds(b, 1), :].astype(jnp.float32)
+            now = rank[:, pl.ds(pl.multiple_of(b * width, width), width)]
+            src_ref[b] = (now * (1.0 - dead)).astype(src_ref.dtype)
+            return mass + now * dead
+
+        mass_ref[...] = lax.fori_loop(0, part, one, mass_ref[...], unroll=4)
 
     @pl.loop(1, count)
     def _(d):
         copy(d).wait()
 
 
-def bcast(stat, count):
+def first(request, dang, rank, blocks, width, count):
+    seed_cols = rank.shape[0]
     return pl.pallas_call(
-        functools.partial(bcast_kernel, count),
-        out_shape=jax.ShapeDtypeStruct((count,) + stat.shape, stat.dtype),
+        functools.partial(first_kernel, count),
+        out_shape=(
+            jax.ShapeDtypeStruct((count,) + request.shape, request.dtype),
+            jax.ShapeDtypeStruct((blocks, seed_cols, width), jnp.bfloat16),
+            jax.ShapeDtypeStruct((seed_cols, width), jnp.float32),
+        ),
+        in_specs=[WHOLE, WHOLE, FAR],
+        out_specs=(WHOLE, WHOLE, WHOLE),
+        scratch_shapes=[
+            pltpu.VMEM(rank.shape, rank.dtype),
+            pltpu.SemaphoreType.DMA((CHUNKS,)),
+            pltpu.SemaphoreType.DMA((count,)),
+            pltpu.SemaphoreType.DMA((count,)),
+        ],
+        compiler_params=pltpu.CompilerParams(
+            collective_id=1, has_side_effects=True, vmem_limit_bytes=FIRST_BYTES
+        ),
+        name="first_source",
+    )(request, dang, rank)
+
+
+def last_kernel(count, groups, stat_ref, mine_ref, whole_ref, tiles, send_sem, recv_sem):
+    total = count * groups
+    group = lax.axis_index("seed")
+    me = group * count + lax.axis_index("dom")
+    barrier = pltpu.get_barrier_semaphore()
+
+    def device(k):
+        peer = lax.rem(me + k, total)
+        return {"dom": lax.rem(peer, count), "seed": peer // count}
+
+    @pl.loop(1, total)
+    def _(k):
+        pl.semaphore_signal(barrier, inc=1, device_id=device(k), device_id_type=MESH)
+
+    pl.semaphore_wait(barrier, total - 1)
+
+    def copy(k):
+        return pltpu.make_async_remote_copy(
+            src_ref=stat_ref,
+            dst_ref=tiles.at[me],
+            send_sem=send_sem.at[k],
+            recv_sem=recv_sem.at[k],
+            device_id=device(k),
+            device_id_type=MESH,
+        )
+
+    @pl.loop(1, total)
+    def _(k):
+        copy(k).start()
+
+    tiles[me] = stat_ref[...]
+
+    @pl.loop(1, total)
+    def _(k):
+        copy(k).wait()
+
+    def added(first, end):
+        zero = jnp.zeros(stat_ref.shape, stat_ref.dtype)
+        return lax.fori_loop(0, end, lambda i, t: t + tiles[first + i], zero)
+
+    mine_ref[...] = added(group * count, count)
+    whole_ref[...] = added(0, total)
+
+
+def last(stat, count, groups):
+    total = count * groups
+    tile = jax.ShapeDtypeStruct(stat.shape, stat.dtype)
+    return pl.pallas_call(
+        functools.partial(last_kernel, count, groups),
+        out_shape=(tile, tile),
         in_specs=[WHOLE],
-        out_specs=WHOLE,
-        scratch_shapes=[pltpu.SemaphoreType.DMA((count,)), pltpu.SemaphoreType.DMA((count,))],
-        compiler_params=pltpu.CompilerParams(collective_id=1, has_side_effects=True),
-        name="bcast_stats",
+        out_specs=(WHOLE, WHOLE),
+        scratch_shapes=[
+            pltpu.VMEM((total,) + stat.shape, stat.dtype),
+            pltpu.SemaphoreType.DMA((total,)),
+            pltpu.SemaphoreType.DMA((total,)),
+        ],
+        compiler_params=pltpu.CompilerParams(collective_id=2, has_side_effects=True),
+        name="last_sums",
     )(stat)
 
 
@@ -230,37 +327,15 @@
     )(wanted, src, stat, band)
 
 
-def init_kernel(rank_ref, dang_ref, src_ref, stat_ref):
-    blocks, seed_cols, width = src_ref.shape
-
-    def step(b, mass):
-        dead = dang_ref[pl.ds(b, 1), :].astype(jnp.float32)
-        rank = rank_ref[:, pl.ds(pl.multiple_of(b * width, width), width)]
-        src_ref[b] = (rank * (1.0 - dead)).astype(src_ref.dtype)
-        return mass + rank * dead
-
-    mass = lax.fori_loop(0, blocks, step, jnp.zeros((seed_cols, width), jnp.float32), unroll=4)
-    stat_ref[...] = columns_to_rows([jnp.sum(mass, axis=1, keepdims=True)], seed_cols)
-
-
-def init(rank, dang, blocks, width):
-    return pl.pallas_call(
-        init_kernel,
-        out_shape=(
-            jax.ShapeDtypeStruct((blocks, rank.shape[0], width), jnp.bfloat16),
-            jax.ShapeDtypeStruct((STAT_ROWS, LANES), jnp.float32),
-        ),
-        in_specs=[WHOLE, WHOLE],
-        out_specs=(WHOLE, WHOLE),
-        compiler_params=pltpu.CompilerParams(vmem_limit_bytes=EXCHANGE_BYTES),
-        name="first_source",
-    )(rank, dang)
-
-
 def step_kernel(
-    vertices, slot_ref, row_ref, place_ref, off_hbm, rank_ref, part_ref, fetched_ref,
-    all_ref, dang_ref, seed_ref, rank_out, src_out, stat_out, off, acc, off_sem,
+    vertices, iteration, final, slot_ref, row_ref, place_ref, off_hbm, rank_ref, part_ref, fetched_ref,
+    all_ref, dang_ref, seed_ref, stat_ref, rank_out, *rest,
 ):
+    if final:
+        stat_out, off, acc, off_sem, rank_new, rank_sem = rest
+    else:
+        src_out, stat_out, off, acc, off_sem = rest
+        rank_new = rank_out
     blocks, seed_cols, width = part_ref.shape
     slots = off.shape[0]
     off_part = slots // CHUNKS
@@ -310,8 +385,9 @@
         is_seed = seeds == b * width
         rank = rank_ref[:, here]
         updated = DAMP * (acc[b] + mass) + jnp.where(is_seed, 1.0 - DAMP, 0.0)
-        rank_out[:, here] = updated
-        src_out[b] = (updated * (1.0 - dead)).astype(src_out.dtype)
+        rank_new[:, here] = updated
+        if not final:
+            src_out[b] = (updated * (1.0 - dead)).astype(src_out.dtype)
         return (
             dead_mass + updated * dead,
             moved + jnp.abs(updated - rank),
@@ -319,33 +395,50 @@
         )
 
     nothing = jnp.zeros((seed_cols, width), jnp.float32)
-    sums = lax.fori_loop(0, blocks, finish, (nothing, nothing, nothing), unroll=2)
-    stat_out[...] = columns_to_rows([jnp.sum(s, axis=1, keepdims=True) for s in sums], seed_cols)
-
-
-def step(vertices, slot, row, place, off, rank, part, fetched, stats, dang, seeds):
+    part = blocks // CHUNKS
+
+    def rank_copy(c):
+        here = pl.ds(c * part * width, part * width)
+        return pltpu.make_async_copy(rank_new.at[:, here], rank_out.at[:, here], rank_sem.at[c])
+
+    sums = (nothing, nothing, nothing)
+    for c in range(CHUNKS):
+        sums = lax.fori_loop(c * part, (c + 1) * part, finish, sums, unroll=4)
+        if final:
+            rank_copy(c).start()
+    mass, moved, own = [jnp.sum(s, axis=1, keepdims=True) for s in sums]
+    rows = columns_to_rows({0: mass, 1: own, 2 + iteration: moved}, seed_cols)
+    kind = lax.broadcasted_iota(jnp.int32, rows.shape, 0)
+    stat_out[...] = rows + jnp.where(kind >= 2, stat_ref[...], 0.0)
+    if final:
+        for c in range(CHUNKS):
+            rank_copy(c).wait()
+
+
+def step(vertices, iteration, slot, row, place, off, rank, part, fetched, stats, dang, seeds, stat):
+    final = iteration == ITERS - 1
     blocks, seed_cols, width = part.shape
     flops = 2 * seed_cols * width * width * off.shape[0]
+    rank_type = jax.ShapeDtypeStruct(rank.shape, rank.dtype)
+    src_type = jax.ShapeDtypeStruct(part.shape, fetched.dtype)
+    stat_type = jax.ShapeDtypeStruct(stat.shape, stat.dtype)
     return pl.pallas_call(
-        functools.partial(step_kernel, vertices),
-        out_shape=(
-            jax.ShapeDtypeStruct(rank.shape, rank.dtype),
-            jax.ShapeDtypeStruct(part.shape, fetched.dtype),
-            jax.ShapeDtypeStruct((STAT_ROWS, LANES), jnp.float32),
-        ),
-        in_specs=[SCALARS, SCALARS, SCALARS, FAR] + [WHOLE] * 6,
-        out_specs=(WHOLE, WHOLE, WHOLE),
+        functools.partial(step_kernel, vertices, iteration, final),
+        out_shape=(rank_type, stat_type) if final else (rank_type, src_type, stat_type),
+        in_specs=[SCALARS, SCALARS, SCALARS, FAR] + [WHOLE] * 7,
+        out_specs=(FAR, WHOLE) if final else (WHOLE, WHOLE, WHOLE),
         scratch_shapes=[
             pltpu.VMEM(off.shape, off.dtype),
             pltpu.VMEM((blocks + 1, seed_cols, width), jnp.float32),
             pltpu.SemaphoreType.DMA((CHUNKS,)),
-        ],
+        ]
+        + ([pltpu.VMEM(rank.shape, rank.dtype), pltpu.SemaphoreType.DMA((CHUNKS,))] if final else []),
         compiler_params=pltpu.CompilerParams(vmem_limit_bytes=STEP_BYTES),
         cost_estimate=pl.CostEstimate(
             flops=flops, bytes_accessed=2 * off.size, transcendentals=0
         ),
         name="power_step",
-    )(slot, row, place, off, rank, part, fetched, stats, dang, seeds)
+    )(slot, row, place, off, rank, part, fetched, stats, dang, seeds, stat)
 
 
 def plan_requests(tile_src, tile_count, blocks, count):
@@ -374,30 +467,30 @@
     requests, slot, live = plan_requests(tile_src, tile_count, blocks, count)
     rows = jnp.where(live, tile_row[0], blocks)
     padded = jnp.pad(requests, (0, STAT_ROWS * LANES - count * CAP)).reshape(STAT_ROWS, LANES)
-    asked = bcast(padded.astype(jnp.float32), count)
+    dang = dangling.reshape(blocks, width)
+    asked, src, mass = first(padded.astype(jnp.float32), dang, rank_in, blocks, width, count)
     asked = asked.reshape(count, STAT_ROWS * LANES)
     wanted = lax.dynamic_slice_in_dim(asked, me * CAP, CAP, axis=1)
     wanted = wanted.astype(jnp.int32).reshape(-1)
-
-    dang = dangling.reshape(blocks, width)
+    stat = jnp.pad(
+        jnp.sum(mass, axis=1)[None, :], ((0, STAT_ROWS - 1), (0, LANES - seed_cols))
+    )
+
     seeds = seed_ids[:, None]
     place = jnp.stack([tile_count[0], me.astype(jnp.int32)])
     rank = rank_in
-    src, stat = init(rank, dang, blocks, width)
-    gathered = []
-    for _ in range(ITERS):
+    for iteration in range(ITERS):
         fetched, stats, part = exchange(wanted, src, stat, band_tiles, count)
-        gathered.append(stats)
         fetched = fetched.reshape((count * CAP,) + src.shape[1:])
-        rank, src, stat = step(
-            vertices, slot, rows, place, off_tiles, rank, part, fetched, stats, dang, seeds
-        )
-    gathered.append(bcast(stat, count))
-    moved = jnp.stack([jnp.sum(g[:, 1, :seed_cols], axis=0) for g in gathered[1:]])
-    own = jnp.sum(gathered[-1][:, 2, :seed_cols], axis=0)
-    change = moved / vertices
-    total_change = lax.psum(jnp.sum(change, axis=1), "seed") / (seed_cols * groups)
-    return (rank, change, total_change, own)
+        rank, *src, stat = step(
+            vertices, iteration, slot, rows, place, off_tiles, rank, part, fetched, stats, dang,
+            seeds, stat,
+        )
+        src = src[0] if src else None
+    mine, whole = last(stat, count, groups)
+    change = mine[2 : 2 + ITERS, :seed_cols] / vertices
+    total_change = jnp.sum(whole[2 : 2 + ITERS], axis=1) / vertices / (seed_cols * groups)
+    return (rank, change, total_change, mine[1, :seed_cols])
 
 
 def solution(mesh):

time: 152 us -> 139 us (0.914); the launches traced: 153 us -> 137 us
  Pallas kernels: 139 us -> 128 us
  blocking collectives: 2.46 us -> 0 us
  local copies, waits for them, and re-layouts: 5.43 us -> 3.64 us
    pallas_call x6 -> x5, Pallas kernels: 71.6 us -> 65.6 us  [the longest x3 42.5 us: step(): pl.pallas_call(functools.partial(step_kernel, vertices, iteration, final)...]
    pallas_call x3, Pallas kernels: 67.2 us -> 62.1 us  [exchange(): pl.pallas_call(functools.partial(exchange_kernel, count), out_shape=(jax....]
    unnamed x9, local copies, waits for them, and re-layouts: 4.43 us -> 1.45 us
    psum x1 -> x0, blocking collectives: 2.46 us -> none  [on_device(): lax.psum(jnp.sum(change, axis=1), 'seed') / (seed_cols * groups)]
where the time goes in v3:
time: 139 us; the launch traced here: 137 us
  Pallas kernels  128 us (92%)
  other arithmetic  4.47 us (3%)
  local copies, waits for them, and re-layouts  3.64 us (3%)
  between operations  1.42 us (1%)
    pallas_call x3, Pallas kernels, exchange(): pl.pallas_call(functools.partial(exchange_kernel, count), out_shape=(jax....  62.1 us
    pallas_call x3, Pallas kernels, step(): pl.pallas_call(functools.partial(step_kernel, vertices, iteration, final)...  42.5 us
    pallas_call x1, Pallas kernels, last(): pl.pallas_call(functools.partial(last_kernel, count, groups), out_shape=(...  13.3 us
    pallas_call x1, Pallas kernels, first(): pl.pallas_call(functools.partial(first_kernel, count), out_shape=(jax.Sha...  9.84 us

profile of v3, /device:TPU:0, one launch (start us, length us, event | category | flops | bytes accessed | tf_op | source)
XLA Modules:
  0.0 137.3 jit_solution(18438997006387649392)
XLA Ops:
  1.3 0.1 pad_add_fusion.1.place_ref
  1.4 0.7 multiply_subtract_fusion
  2.1 0.1 select_reduce_fusion
  2.2 0.1 select_reduce_fusion.1
  2.3 0.7 convert_add_fusion
  3.0 0.1 copy.20
  3.1 0.1 reshape.36
  3.2 0.7 copy.21.seed_ref
  3.9 0.0 copy-start.1
  3.9 0.8 copy-done.1
  4.8 9.8 %first_source.1 = (f32[16,8,128]{2,1,0:T(8,128)S(1)}, bf16[128,64,128]{2,1,0:T(8,128)(2,1)S(1)}, f32[64,128]{1,0:T(8,128)S(1)}) custom-call(f32[8,128]{1,0:T(8,128)S(1)} %convert_bitcast_fusion.request_ref, s32[128,128]{1,0:T(8,128)S(1)} %bitcast.24, f32[64,16384]{1,0:T(8,128)} %rank_ref.1), custom_call_target="tpu_custom_call" | custom-call | tf_op jit(solution)/shard_map/first_source/pallas_call | solution.py:111
  14.6 0.1 dynamic-slice_convert_fusion
  14.7 0.1 reshape.39.wanted_ref
  14.8 0.1 reduce_sum.28
  14.9 0.0 copy-start
  14.9 0.0 copy-start.2
  15.0 20.9 %exchange_blocks.3 = (bf16[16,2,64,128]{3,2,1,0:T(8,128)(2,1)S(1)}, f32[16,8,128]{2,1,0:T(8,128)S(1)}, f32[128,64,128]{2,1,0:T(8,128)S(1)}) custom-call(s32[32]{0:T(128)S(1)} %reshape.39.wanted_ref, bf16[128,64,128]{2,1,0:T(8,128)(2,1)S(1)} %get-tuple-element.27.src_ref, f32[8,128]{1,0:T(8,128)S(1)} %pad.9.stat_ref, bf16[128,3,128,128]{3,2,1,0:T(8,128)(2,1)} %band_hbm.5), custom_call_target="tpu_custom_call" | custom-call | flops 805306368 | bytes 12582912 | tf_op jit(solution)/shard_map/exchange_blocks/pallas_call | solution.py:304
  35.9 0.0 copy-done
  35.9 0.0 copy-done.2
  35.9 14.0 %power_step.3 = (f32[64,16384]{1,0:T(8,128)S(1)}, bf16[128,64,128]{2,1,0:T(8,128)(2,1)S(1)}, f32[8,128]{1,0:T(8,128)S(1)}) custom-call(s32[512]{0:T(512)S(1)} %get-tuple-element.52.slot_ref, s32[512]{0:T(512)S(1)} %get-tuple-element.53.row_ref, s32[2]{0:T(128)S(1)} %pad_add_fusion.1.place_ref, bf16[512,128,128]{2,1,0:T(8,128)(2,1)} %off_hbm.5, ...), custom_call_target="tpu_custom_call" | custom-call | flops 1073741824 | bytes 16777216 | tf_op jit(solution)/shard_map/power_step/pallas_call | solution.py:425
  49.9 20.3 %exchange_blocks.4 = (bf16[16,2,64,128]{3,2,1,0:T(8,128)(2,1)S(1)}, f32[16,8,128]{2,1,0:T(8,128)S(1)}, f32[128,64,128]{2,1,0:T(8,128)S(1)}) custom-call(s32[32]{0:T(128)S(1)} %reshape.39.wanted_ref, bf16[128,64,128]{2,1,0:T(8,128)(2,1)S(1)} %get-tuple-element.33.src_ref, f32[8,128]{1,0:T(8,128)S(1)} %get-tuple-element.34.stat_ref, ...), custom_call_target="tpu_custom_call" | custom-call | flops 805306368 | bytes 12582912 | tf_op jit(solution)/shard_map/exchange_blocks/pallas_call | solution.py:304
  70.2 14.0 %power_step.4 = (f32[64,16384]{1,0:T(8,128)S(1)}, bf16[128,64,128]{2,1,0:T(8,128)(2,1)S(1)}, f32[8,128]{1,0:T(8,128)S(1)}) custom-call(s32[512]{0:T(512)S(1)} %get-tuple-element.52.slot_ref, s32[512]{0:T(512)S(1)} %get-tuple-element.53.row_ref, s32[2]{0:T(128)S(1)} %pad_add_fusion.1.place_ref, bf16[512,128,128]{2,1,0:T(8,128)(2,1)} %off_hbm.5, ...), custom_call_target="tpu_custom_call" | custom-call | flops 1073741824 | bytes 16777216 | tf_op jit(solution)/shard_map/power_step/pallas_call | solution.py:425
  84.2 20.9 %exchange_blocks.5 = (bf16[16,2,64,128]{3,2,1,0:T(8,128)(2,1)S(1)}, f32[16,8,128]{2,1,0:T(8,128)S(1)}, f32[128,64,128]{2,1,0:T(8,128)S(1)}) custom-call(s32[32]{0:T(128)S(1)} %reshape.39.wanted_ref, bf16[128,64,128]{2,1,0:T(8,128)(2,1)S(1)} %get-tuple-element.39.src_ref, f32[8,128]{1,0:T(8,128)S(1)} %get-tuple-element.40.stat_ref, ...), custom_call_target="tpu_custom_call" | custom-call | flops 805306368 | bytes 12582912 | tf_op jit(solution)/shard_map/exchange_blocks/pallas_call | solution.py:304
  105.1 14.4 %power_step.5 = (f32[64,16384]{1,0:T(8,128)}, f32[8,128]{1,0:T(8,128)S(1)}) custom-call(s32[512]{0:T(512)S(1)} %get-tuple-element.52.slot_ref, s32[512]{0:T(512)S(1)} %get-tuple-element.53.row_ref, s32[2]{0:T(128)S(1)} %pad_add_fusion.1.place_ref, bf16[512,128,128]{2,1,0:T(8,128)(2,1)} %off_hbm.5, f32[64,16384]{1,0:T(8,128)S(1)} %get-tuple-element.38.rank_ref, ...), custom_call_target="tpu_custom_call" | custom-call | flops 1073741824 | bytes 16777216 | tf_op jit(solution)/shard_map/power_step/pallas_call | solution.py:425
  119.6 0.0 copy-start.3
  119.6 0.6 copy-done.3
  120.2 13.3 %last_sums.1 = (f32[8,128]{1,0:T(8,128)}, f32[8,128]{1,0:T(8,128)}) custom-call(f32[8,128]{1,0:T(8,128)} %copy-done.3), custom_call_target="tpu_custom_call" | custom-call | tf_op jit(solution)/shard_map/last_sums/pallas_call | solution.py:180
  133.5 0.8 slice_reduce_fusion
  134.3 0.5 broadcast_multiply_fusion
  134.8 1.2 slice_bitcast_fusion
  136.0 1.3 slice_multiply_fusion
  (5 shorter events, 0.0 us)
Async XLA Ops:
  3.9 0.8 copy-start.1
  14.9 21.0 %copy-start = (f32[64,16384]{1,0:T(8,128)S(1)}, f32[64,16384]{1,0:T(8,128)}, u32[]{:S(2)}) copy-start(f32[64,16384]{1,0:T(8,128)} %rank_ref.1) | copy-start | bytes 12582916
  14.9 21.0 %copy-start.2 = (s32[16384]{0:T(1024)S(1)}, s32[16384]{0:T(1024)}, u32[]{:S(2)}) copy-start(s32[16384]{0:T(1024)} %param.15) | copy-start | bytes 196612
  119.6 0.6 copy-start.3

commit v4 on v3

--- a/solution.py
+++ b/solution.py
@@ -12,9 +12,8 @@
 DAMP = 0.85
 LANES = 128
 STAT_ROWS = 8
-GROUP = 32
+GROUP = 64
 CHUNKS = 8
-EARLY = 1
 STEP_BYTES = 36 * 1024 * 1024
 FIRST_BYTES = 48 * 1024 * 1024
 EXCHANGE_BYTES = 36 * 1024 * 1024
@@ -265,8 +264,6 @@
 
     fetched_ref[me] = jnp.zeros(fetched_ref.shape[1:], fetched_ref.dtype)
     all_ref[me] = stat_ref[...]
-    for c in range(EARLY):
-        band_chunk(c)
     pl.semaphore_wait(pltpu.get_barrier_semaphore(), count - 1)
 
     @pl.loop(1, count)
@@ -280,7 +277,7 @@
     def _(d):
         stat_copy(d).start()
 
-    @pl.loop(EARLY, CHUNKS)
+    @pl.loop(0, CHUNKS)
     def _(c):
         band_chunk(c)
 

time: 139 us -> 138 us (level); the launches traced: 137 us -> 138 us
    pallas_call x3, Pallas kernels: 42.5 us -> 51.9 us  [step(): pl.pallas_call(functools.partial(step_kernel, vertices, iteration, final)...]
    pallas_call x3, Pallas kernels: 62.1 us -> 56.2 us  [exchange(): pl.pallas_call(functools.partial(exchange_kernel, count), out_shape=(jax....]
    pallas_call x1, Pallas kernels: 13.3 us -> 10.5 us  [last(): pl.pallas_call(functools.partial(last_kernel, count, groups), out_shape=(...]
where the time goes in v4:
time: 138 us
  Pallas kernels  128 us (93%)
  other arithmetic  4.47 us (3%)
  local copies, waits for them, and re-layouts  3.64 us (3%)
  between operations  1.42 us (1%)
    pallas_call x3, Pallas kernels, exchange(): pl.pallas_call(functools.partial(exchange_kernel, count), out_shape=(jax....  56.2 us
    pallas_call x3, Pallas kernels, step(): pl.pallas_call(functools.partial(step_kernel, vertices, iteration, final)...  51.9 us
    pallas_call x1, Pallas kernels, last(): pl.pallas_call(functools.partial(last_kernel, count, groups), out_shape=(...  10.5 us
    pallas_call x1, Pallas kernels, first(): pl.pallas_call(functools.partial(first_kernel, count), out_shape=(jax.Sha...  9.84 us

profile of v4, /device:TPU:0, one launch (start us, length us, event | category | flops | bytes accessed | tf_op | source)
XLA Modules:
  0.0 138.0 jit_solution(2235104666454875531)
XLA Ops:
  1.3 0.1 pad_add_fusion.1.place_ref
  1.4 0.7 multiply_subtract_fusion
  2.1 0.1 select_reduce_fusion
  2.2 0.1 select_reduce_fusion.1
  2.3 0.7 convert_add_fusion
  3.0 0.1 copy.20
  3.1 0.1 reshape.36
  3.2 0.7 copy.21.seed_ref
  3.9 0.0 copy-start.1
  3.9 0.8 copy-done.1
  4.8 9.8 %first_source.1 = (f32[16,8,128]{2,1,0:T(8,128)S(1)}, bf16[128,64,128]{2,1,0:T(8,128)(2,1)S(1)}, f32[64,128]{1,0:T(8,128)S(1)}) custom-call(f32[8,128]{1,0:T(8,128)S(1)} %convert_bitcast_fusion.request_ref, s32[128,128]{1,0:T(8,128)S(1)} %bitcast.24, f32[64,16384]{1,0:T(8,128)} %rank_ref.1), custom_call_target="tpu_custom_call" | custom-call | tf_op jit(solution)/shard_map/first_source/pallas_call | solution.py:110
  14.6 0.1 dynamic-slice_convert_fusion
  14.7 0.1 reshape.39.wanted_ref
  14.8 0.1 reduce_sum.28
  14.9 0.0 copy-start
  14.9 0.0 copy-start.2
  15.0 19.3 %exchange_blocks.3 = (bf16[16,2,64,128]{3,2,1,0:T(8,128)(2,1)S(1)}, f32[16,8,128]{2,1,0:T(8,128)S(1)}, f32[128,64,128]{2,1,0:T(8,128)S(1)}) custom-call(s32[32]{0:T(128)S(1)} %reshape.39.wanted_ref, bf16[128,64,128]{2,1,0:T(8,128)(2,1)S(1)} %get-tuple-element.27.src_ref, f32[8,128]{1,0:T(8,128)S(1)} %pad.9.stat_ref, bf16[128,3,128,128]{3,2,1,0:T(8,128)(2,1)} %band_hbm.5), custom_call_target="tpu_custom_call" | custom-call | flops 805306368 | bytes 12582912 | tf_op jit(solution)/shard_map/exchange_blocks/pallas_call | solution.py:301
  34.2 0.0 copy-done
  34.3 0.0 copy-done.2
  34.3 17.2 %power_step.3 = (f32[64,16384]{1,0:T(8,128)S(1)}, bf16[128,64,128]{2,1,0:T(8,128)(2,1)S(1)}, f32[8,128]{1,0:T(8,128)S(1)}) custom-call(s32[512]{0:T(512)S(1)} %get-tuple-element.52.slot_ref, s32[512]{0:T(512)S(1)} %get-tuple-element.53.row_ref, s32[2]{0:T(128)S(1)} %pad_add_fusion.1.place_ref, bf16[512,128,128]{2,1,0:T(8,128)(2,1)} %off_hbm.5, ...), custom_call_target="tpu_custom_call" | custom-call | flops 1073741824 | bytes 16777216 | tf_op jit(solution)/shard_map/power_step/pallas_call | solution.py:422
  51.4 19.0 %exchange_blocks.4 = (bf16[16,2,64,128]{3,2,1,0:T(8,128)(2,1)S(1)}, f32[16,8,128]{2,1,0:T(8,128)S(1)}, f32[128,64,128]{2,1,0:T(8,128)S(1)}) custom-call(s32[32]{0:T(128)S(1)} %reshape.39.wanted_ref, bf16[128,64,128]{2,1,0:T(8,128)(2,1)S(1)} %get-tuple-element.33.src_ref, f32[8,128]{1,0:T(8,128)S(1)} %get-tuple-element.34.stat_ref, ...), custom_call_target="tpu_custom_call" | custom-call | flops 805306368 | bytes 12582912 | tf_op jit(solution)/shard_map/exchange_blocks/pallas_call | solution.py:301
  70.4 17.2 %power_step.4 = (f32[64,16384]{1,0:T(8,128)S(1)}, bf16[128,64,128]{2,1,0:T(8,128)(2,1)S(1)}, f32[8,128]{1,0:T(8,128)S(1)}) custom-call(s32[512]{0:T(512)S(1)} %get-tuple-element.52.slot_ref, s32[512]{0:T(512)S(1)} %get-tuple-element.53.row_ref, s32[2]{0:T(128)S(1)} %pad_add_fusion.1.place_ref, bf16[512,128,128]{2,1,0:T(8,128)(2,1)} %off_hbm.5, ...), custom_call_target="tpu_custom_call" | custom-call | flops 1073741824 | bytes 16777216 | tf_op jit(solution)/shard_map/power_step/pallas_call | solution.py:422
  87.6 17.9 %exchange_blocks.5 = (bf16[16,2,64,128]{3,2,1,0:T(8,128)(2,1)S(1)}, f32[16,8,128]{2,1,0:T(8,128)S(1)}, f32[128,64,128]{2,1,0:T(8,128)S(1)}) custom-call(s32[32]{0:T(128)S(1)} %reshape.39.wanted_ref, bf16[128,64,128]{2,1,0:T(8,128)(2,1)S(1)} %get-tuple-element.39.src_ref, f32[8,128]{1,0:T(8,128)S(1)} %get-tuple-element.40.stat_ref, ...), custom_call_target="tpu_custom_call" | custom-call | flops 805306368 | bytes 12582912 | tf_op jit(solution)/shard_map/exchange_blocks/pallas_call | solution.py:301
  105.5 17.6 %power_step.5 = (f32[64,16384]{1,0:T(8,128)}, f32[8,128]{1,0:T(8,128)S(1)}) custom-call(s32[512]{0:T(512)S(1)} %get-tuple-element.52.slot_ref, s32[512]{0:T(512)S(1)} %get-tuple-element.53.row_ref, s32[2]{0:T(128)S(1)} %pad_add_fusion.1.place_ref, bf16[512,128,128]{2,1,0:T(8,128)(2,1)} %off_hbm.5, f32[64,16384]{1,0:T(8,128)S(1)} %get-tuple-element.38.rank_ref, ...), custom_call_target="tpu_custom_call" | custom-call | flops 1073741824 | bytes 16777216 | tf_op jit(solution)/shard_map/power_step/pallas_call | solution.py:422
  123.1 0.0 copy-start.3
  123.1 0.6 copy-done.3
  123.7 10.5 %last_sums.1 = (f32[8,128]{1,0:T(8,128)}, f32[8,128]{1,0:T(8,128)}) custom-call(f32[8,128]{1,0:T(8,128)} %copy-done.3), custom_call_target="tpu_custom_call" | custom-call | tf_op jit(solution)/shard_map/last_sums/pallas_call | solution.py:179
  134.2 0.8 slice_reduce_fusion
  135.0 0.5 broadcast_multiply_fusion
  135.5 1.2 slice_bitcast_fusion
  136.7 1.3 slice_multiply_fusion
  (5 shorter events, 0.0 us)
Async XLA Ops:
  3.9 0.8 copy-start.1
  14.9 19.3 %copy-start = (f32[64,16384]{1,0:T(8,128)S(1)}, f32[64,16384]{1,0:T(8,128)}, u32[]{:S(2)}) copy-start(f32[64,16384]{1,0:T(8,128)} %rank_ref.1) | copy-start | bytes 12582916
  14.9 19.3 %copy-start.2 = (s32[16384]{0:T(1024)S(1)}, s32[16384]{0:T(1024)}, u32[]{:S(2)}) copy-start(s32[16384]{0:T(1024)} %param.15) | copy-start | bytes 196612
  123.1 0.6 copy-start.3
